TPU v7x, 512 devices: a whole 4x4x16 slice. The times are simulated.
512 devices in a mesh: seg: 32 (over z_lo, x), bank: 16 (over y, z_hi, core).
Axes of the slice: x: 4, y: 4, z: 16 (z_hi: 2, z_lo: 8; z = z_hi * 8 + z_lo), core: 2. Of those that a mesh axis runs over, the one named last changes fastest.
Arguments:
- strain: float32 [1572864], P('seg'), may hold values from -24000 to 24000, as said below
- inv_asd: float32 [32768], replicated, may hold values from 0.3 to 3
- templates: bfloat16 [2, 32, 32768], P(None, 'bank'), may hold values from -6 to 6
- tmpl_len: int32 [32], P('bank'), may hold values from 2048 to 16384, as said below
- weights: float32 [32], P('bank'), may hold values from 0.2 to 5
- chirp_mass: float32 [32], P('bank'), may hold values from 10 to 60
- valid: int32 [1536], P('seg'), may hold values 0 or 1
Outputs:
- log_like: float32 [1572864], P(('seg', 'bank'))
- chirp_mean: float32 [1572864], P(('seg', 'bank'))
- delay_mean: float32 [1572864], P(('seg', 'bank'))
Inputs may be any that keep to these rules, and one draw needn't show every extreme that they name: `strain`: noise amplitude may change from one block of 1024 samples to the next. `tmpl_len`: template lengths lie between 2048 and 16384 samples, both ends taken.
All inputs are finite; a program needn't handle non-finite values. No bound on the sum of `valid` on one device may be relied on, other than what follows from the above.
Results may differ from a plain program's by a relative error of at most 0.00035.
Values sent between devices are 32-bit elements; how exact they have to be, the bound alone decides.
A program may use at most 64 MiB of HBM per device.

v0:
```python
import math

import jax
import jax.numpy as jnp
from jax import lax
from jax.sharding import PartitionSpec as P

NFFT = 65536
FA = 256
OVER = 16384
RATE = 4096
HOP = 49152


HIGH = lax.Precision.HIGHEST


def passed_along(array, axis, by):
    length = lax.axis_size(axis)
    pairs = [(i, i + by) for i in range(length) if 0 <= i + by < length]
    return lax.ppermute(array, axis, pairs)


def log_bessel(rho_val):
    small_x = jnp.minimum(rho_val, 3.75)
    small_t = (small_x / 3.75) ** 2
    small_poly = 1.0 + small_t * (
        3.5156229
        + small_t
        * (
            3.0899424
            + small_t
            * (1.2067492 + small_t * (0.2659732 + small_t * (0.0360768 + small_t * 0.0045813)))
        )
    )
    large_x = jnp.maximum(rho_val, 3.75)
    large_q = 3.75 / large_x
    large_poly = 0.39894228 + large_q * (
        0.01328592
        + large_q
        * (
            0.00225319
            + large_q
            * (
                -0.00157565
                + large_q
                * (
                    0.00916281
                    + large_q
                    * (
                        -0.02057706
                        + large_q * (0.02635537 + large_q * (-0.01647633 + large_q * 0.00392377))
                    )
                )
            )
        )
    )
    large_val = large_x - 0.5 * jnp.log(large_x) + jnp.log(large_poly)
    return jnp.where(rho_val < 3.75, jnp.log(small_poly), large_val)


def phase_table(row_count, col_count, period):
    index_grid = (
        jnp.arange(row_count, dtype=jnp.int32)[:, None]
        * jnp.arange(col_count, dtype=jnp.int32)[None, :]
        % period
    )
    angles = index_grid.astype(jnp.float32) * (2.0 * math.pi / period)
    return (jnp.cos(angles), jnp.sin(angles))


def contract_last(left_mat, right_mat):
    return lax.dot_general(
        left_mat,
        right_mat,
        (((1,), (1,)), ((), ())),
        precision=HIGH,
        preferred_element_type=jnp.float32,
    )


def pick_row(score_row, begin_at):
    return lax.dynamic_slice_in_dim(score_row, begin_at, HOP)


def finish(peak_score, total, chirp_sum, delay_sum, prior_sum):
    return (peak_score + jnp.log(total) - jnp.log(prior_sum), chirp_sum / total, delay_sum / total)


def local(strain, inv_asd, templates, tmpl_len, weights, chirp_mass, valid):
    hop_len = strain.shape[0]
    block_count = valid.shape[0]
    fb_len = NFFT // FA
    half_rows = fb_len // 2
    local_count = templates.shape[1]
    gated_data = (
        strain.reshape(block_count, hop_len // block_count) * valid.astype(jnp.float32)[:, None]
    ).reshape(hop_len)
    earlier = passed_along(gated_data[hop_len - OVER :], "seg", 1)
    window = jnp.concatenate([earlier, gated_data])
    frame_rows = window.reshape(FA, fb_len)
    short_cos, short_sin = phase_table(FA, FA, FA)
    twist_cos, twist_sin = phase_table(FA, fb_len, NFFT)
    long_cos, long_sin = phase_table(half_rows, fb_len, fb_len)
    section_re = jnp.dot(short_cos, frame_rows, precision=HIGH, preferred_element_type=jnp.float32)
    section_im = -jnp.dot(short_sin, frame_rows, precision=HIGH, preferred_element_type=jnp.float32)
    turned_re = section_re * twist_cos + section_im * twist_sin
    turned_im = section_im * twist_cos - section_re * twist_sin
    bin_scale = inv_asd.reshape(half_rows, FA) / math.sqrt(NFFT)
    spec_re = (contract_last(long_cos, turned_re) + contract_last(long_sin, turned_im)) * bin_scale
    spec_im = (contract_last(long_cos, turned_im) - contract_last(long_sin, turned_re)) * bin_scale
    tmpl_re = templates[0].astype(jnp.float32).reshape(local_count, half_rows, FA)
    tmpl_im = templates[1].astype(jnp.float32).reshape(local_count, half_rows, FA)
    asd_sq = (inv_asd * inv_asd).reshape(half_rows, FA)
    sigma_sq = jnp.sum(asd_sq[None] * (tmpl_re * tmpl_re + tmpl_im * tmpl_im), axis=(1, 2))
    prod_re = spec_re[None] * tmpl_re + spec_im[None] * tmpl_im
    prod_im = spec_im[None] * tmpl_re - spec_re[None] * tmpl_im
    inner_re = jnp.einsum("kab,ac->kbc", prod_re, long_cos, precision=HIGH) - jnp.einsum(
        "kab,ac->kbc", prod_im, long_sin, precision=HIGH
    )
    inner_im = jnp.einsum("kab,ac->kbc", prod_re, long_sin, precision=HIGH) + jnp.einsum(
        "kab,ac->kbc", prod_im, long_cos, precision=HIGH
    )
    twisted_re = inner_re * twist_cos[None] - inner_im * twist_sin[None]
    twisted_im = inner_re * twist_sin[None] + inner_im * twist_cos[None]
    corr_re = (
        jnp.einsum("tb,kbc->ktc", short_cos, twisted_re, precision=HIGH)
        - jnp.einsum("tb,kbc->ktc", short_sin, twisted_im, precision=HIGH)
    ).reshape(local_count, NFFT)
    corr_im = (
        jnp.einsum("tb,kbc->ktc", short_cos, twisted_im, precision=HIGH)
        + jnp.einsum("tb,kbc->ktc", short_sin, twisted_re, precision=HIGH)
    ).reshape(local_count, NFFT)
    rho_val = jnp.sqrt((corr_re * corr_re + corr_im * corr_im) / sigma_sq[:, None])
    scores = log_bessel(rho_val)
    starts = OVER - tmpl_len
    aligned = jax.vmap(pick_row)(scores, starts)
    delays = tmpl_len.astype(jnp.float32) / RATE
    bank_count = lax.axis_size("bank")
    traits = jnp.stack([weights, chirp_mass, delays], axis=1)
    traits_rep = jnp.tile(traits, (1, bank_count))
    bank_scores, bank_traits = (
        lax.all_to_all(aligned, "bank", split_axis=1, concat_axis=0, tiled=True),
        lax.all_to_all(traits_rep, "bank", split_axis=1, concat_axis=0, tiled=True),
    )
    all_weights = bank_traits[:, 0]
    peak_score = jnp.max(bank_scores, axis=0)
    masses = all_weights[:, None] * jnp.exp(bank_scores - peak_score[None, :])
    total = jnp.sum(masses, axis=0)
    chirp_sum = jnp.sum(masses * bank_traits[:, 1][:, None], axis=0)
    delay_sum = jnp.sum(masses * bank_traits[:, 2][:, None], axis=0)
    return finish(peak_score, total, chirp_sum, delay_sum, jnp.sum(all_weights))


def solution(mesh):
    placed = (P("seg"), P(), P(None, "bank", None), P("bank"), P("bank"), P("bank"), P("seg"))
    return jax.shard_map(
        local,
        mesh=mesh,
        in_specs=placed,
        out_specs=(P(("seg", "bank")), P(("seg", "bank")), P(("seg", "bank"))),
        check_vma=False,
    )
```

profile of v0, /device:TPU:34, one launch (start us, length us, event | category | flops | bytes accessed | tf_op | source)
XLA Modules:
  0.0 117.1 jit_solution(5144683038463420493)
XLA Ops:
  2.4 3.4 %collective-permute-start = (f32[16384]{0:T(1024)S(1)}, f32[16384]{0:T(1024)S(1)}, u32[]{:S(2)}, u32[]{:S(2)}) collective-permute-start(f32[16384]{0:T(1024)S(1)} %bitcast.74), channel_id=1, source_target_pairs={{0,16},{16,32},{32,48},{48,64},{64,80},{80,96},{96,112},{112,128},... | collective-permute-start | bytes 196616 | tf_op jit(solution)/shard_map/ppermute | solution.py:21
  7.3 16.9 %all-to-all-start.1 = ((f32[2,16,3]{2,0,1:T(2,128)}), f32[2,16,3]{2,0,1:T(2,128)S(1)}, u32[]{:S(2)}, u32[]{:S(2)}) async-start(f32[2,16,3]{2,0,1:T(2,128)} %tile.2), calls=%async_computation.1 | async-start | bytes 32768 | tf_op jit(solution)/shard_map/all_to_all | solution.py:144
  29.2 1.6 %convolution_negate_fusion = f32[256,256]{1,0:T(8,128)S(1)} fusion(f32[256,256]{1,0:T(8,128)S(1)} %reshape.125), kind=kOutput, calls=%fused_computation.9 | convolution fusion | flops 202309632 | bytes 524288 | tf_op jit(solution)/shard_map/dot_general | solution.py:106
  30.9 1.8 %fusion.39 = f32[256,256]{1,0:T(8,128)S(1)} fusion(f32[256,256]{1,0:T(8,128)S(1)} %reshape.125), kind=kOutput, calls=%fused_computation.71 | convolution fusion | flops 202244096 | bytes 524288 | tf_op jit(solution)/shard_map/dot_general | solution.py:105
  32.7 1.9 %fusion.54 = f32[128,256]{1,0:T(8,128)S(1)} fusion(f32[256,256]{1,0:T(8,128)S(1)} %convolution_negate_fusion, f32[256,256]{1,0:T(8,128)S(1)} %fusion.39), kind=kOutput, calls=%fused_computation.82 | convolution fusion | flops 102236160 | bytes 655360 | tf_op jit(solution)/shard_map/dot_general | solution.py:73
  34.5 1.9 %fusion.52 = f32[128,256]{1,0:T(8,128)S(1)} fusion(f32[256,256]{1,0:T(8,128)S(1)} %fusion.39, f32[256,256]{1,0:T(8,128)S(1)} %convolution_negate_fusion), kind=kOutput, calls=%fused_computation.81 | convolution fusion | flops 102236160 | bytes 655360 | tf_op jit(solution)/shard_map/dot_general | solution.py:73
  36.4 1.9 %fusion.5 = f32[128,256]{1,0:T(8,128)S(1)} fusion(f32[128,256]{1,0:T(8,128)S(1)} %div.33, f32[128,256]{1,0:T(8,128)S(1)} %fusion.54, f32[256,256]{1,0:T(8,128)S(1)} %fusion.39, f32[256,256]{1,0:T(8,128)S(1)} %convolution_negate_fusion), kind=kOutput, calls=%fused_computation.13 | convolution fusion | flops 102301696 | bytes 917504 | tf_op jit(solution)/shard_map/dot_general | solution.py:73
  38.4 1.9 %fusion.4 = f32[128,256]{1,0:T(8,128)S(1)} fusion(f32[128,256]{1,0:T(8,128)S(1)} %div.33, f32[128,256]{1,0:T(8,128)S(1)} %fusion.52, f32[256,256]{1,0:T(8,128)S(1)} %convolution_negate_fusion, f32[256,256]{1,0:T(8,128)S(1)} %fusion.39), kind=kOutput, calls=%fused_computation.11 | convolution fusion | flops 102301696 | bytes 917504 | tf_op jit(solution)/shard_map/dot_general | solution.py:73
  40.4 1.1 fusion.31
  41.5 1.1 fusion.27
  42.5 1.1 convolution_subtract_fusion
  43.6 1.1 convolution_add_fusion
  44.7 2.1 %fusion.13 = f32[2,256,256]{2,1,0:T(8,128)S(1)} fusion(f32[2,256,256]{2,1,0:T(8,128)S(1)} %convolution_add_fusion, f32[2,256,256]{2,1,0:T(8,128)S(1)} %convolution_subtract_fusion, f32[256,256]{1,0:T(8,128)S(1)} %get-tuple-element.47, f32[256,256]{1,0:T(8,128)S(1)} %get-tuple-element.48), kind=kOutput, calls=%fused_computation.36 | convolution fusion | flops 403963904 | bytes 2097152 | tf_op jit(solution)/shard_map/tb,kbc->ktc/dot_general | solution.py:131
  46.8 1.9 %fusion.15 = f32[2,256,256]{2,1,0:T(8,128)S(1)} fusion(f32[2,256,256]{2,1,0:T(8,128)S(1)} %convolution_add_fusion, f32[2,256,256]{2,1,0:T(8,128)S(1)} %convolution_subtract_fusion, f32[256,256]{1,0:T(8,128)S(1)} %get-tuple-element.47, f32[256,256]{1,0:T(8,128)S(1)} %get-tuple-element.48), kind=kOutput, calls=%fused_computation.38 | convolution fusion | flops 403963904 | bytes 2097152 | tf_op jit(solution)/shard_map/tb,kbc->ktc/dot_general | solution.py:127
  48.7 1.9 %fusion.3 = f32[2,256,256]{2,1,0:T(8,128)S(1)} fusion(f32[2,256,256]{2,1,0:T(8,128)S(1)} %fusion.15, f32[2,256,256]{2,1,0:T(8,128)S(1)} %convolution_add_fusion, f32[2,256,256]{2,1,0:T(8,128)S(1)} %convolution_subtract_fusion, f32[256,256]{1,0:T(8,128)S(1)} %get-tuple-element.47, f32[256,256]{1,0:T(8,128)S(1)} %get-tuple-element.48), kind=kOutput, calls=%fused_computation.8 | convolution fusion | flops 404226048 | bytes 2621440 | tf_op jit(solution)/shard_map/tb,kbc->ktc/dot_general | solution.py:128
  50.5 1.9 %fusion.2 = f32[2,256,256]{1,2,0:T(8,128)S(1)} fusion(f32[2,256,256]{2,1,0:T(8,128)S(1)} %fusion.3, f32[2,256,256]{2,1,0:T(8,128)S(1)} %fusion.13, f32[2,256,256]{2,1,0:T(8,128)S(1)} %convolution_add_fusion, f32[2,256,256]{2,1,0:T(8,128)S(1)} %convolution_subtract_fusion, f32[256,256]{1,0:T(8,128)S(1)} %get-tuple-element.47, ...), kind=kOutput, calls=%fused_computation.6 | convolution fusion | flops 404357120 | bytes 3145728 | tf_op jit(solution)/shard_map/tb,kbc->ktc/dot_general | solution.py:132
  53.1 3.8 %compare_select_fusion = f32[2,65536]{1,0:T(2,128)S(1)} fusion(f32[2,65536]{1,0:T(2,128)S(1)} %bitcast.66, f32[2]{0:T(128)S(1)} %multiply_reduce_fusion.2), kind=kLoop, calls=%fused_computation.14 | loop fusion | flops 5111808 | bytes 1048584 | tf_op jit(solution)/shard_map/jit(_where)/select_n | solution.py:59
  56.9 13.5 %while.1 = (s32[]{:T(128)}, f32[2,65536]{1,0:T(2,128)S(1)}, s32[2,2]{1,0:T(2,128)S(1)}, f32[2,49152]{1,0:T(2,128)}, s32[]{:T(128)}, /*index=5*/s32[]{:T(128)}) while((s32[]{:T(128)}, f32[2,65536]{1,0:T(2,128)S(1)}, s32[2,2]{1,0:T(2,128)S(1)}, f32[2,49152]{1,0:T(2,128)}, s32[]{:T(128)}, /*index=5*/s32[]{:T(128)}) %tuple.36), condition=%wide.while_cond, body=%wide.while_body.sunk | while | flops 2 | bytes 786545 | solution.py:83
  57.5 1.8 %dynamic-slice.7 = f32[1,49152]{1,0:T(1,128)S(1)} dynamic-slice(f32[2,65536]{1,0:T(2,128)S(1)} %get-tuple-element.91, s32[]{:T(128)} %bitcast.64, s32[]{:T(128)} %bitcast.65), dynamic_slice_sizes={1,49152} | dynamic-slice | bytes 393220 | tf_op jit(solution)/shard_map/vmap()/gather
  59.2 4.4 %dynamic-update-slice.3 = f32[2,49152]{1,0:T(2,128)} dynamic-update-slice(f32[2,49152]{1,0:T(2,128)} %get-tuple-element.87, f32[1,49152]{1,0:T(1,128)S(1)} %dynamic-slice.7, s32[]{:T(128)} %get-tuple-element.84, s32[]{:T(128)} %constant.32.clone.1..sunk) | dynamic-update-slice | bytes 393220 | tf_op jit(solution)/shard_map/vmap()/gather
  64.2 1.8 %dynamic-slice.7 = f32[1,49152]{1,0:T(1,128)S(1)} dynamic-slice(f32[2,65536]{1,0:T(2,128)S(1)} %get-tuple-element.91, s32[]{:T(128)} %bitcast.64, s32[]{:T(128)} %bitcast.65), dynamic_slice_sizes={1,49152} | dynamic-slice | bytes 393220 | tf_op jit(solution)/shard_map/vmap()/gather
  66.0 4.4 %dynamic-update-slice.3 = f32[2,49152]{1,0:T(2,128)} dynamic-update-slice(f32[2,49152]{1,0:T(2,128)} %get-tuple-element.87, f32[1,49152]{1,0:T(1,128)S(1)} %dynamic-slice.7, s32[]{:T(128)} %get-tuple-element.84, s32[]{:T(128)} %constant.32.clone.1..sunk) | dynamic-update-slice | bytes 393220 | tf_op jit(solution)/shard_map/vmap()/gather
  70.4 14.4 %all-to-all-start = ((f32[2,16,3072]{2,0,1:T(2,128)}), f32[2,16,3072]{2,0,1:T(2,128)S(1)}, u32[]{:S(2)}, u32[]{:S(2)}) async-start(f32[2,16,3072]{2,0,1:T(2,128)} %bitcast.6), calls=%async_computation | async-start | bytes 786432 | tf_op jit(solution)/shard_map/all_to_all | solution.py:143
  86.4 29.2 %all-to-all-done = f32[2,16,3072]{2,0,1:T(2,128)S(1)} async-done(((f32[2,16,3072]{2,0,1:T(2,128)}), f32[2,16,3072]{2,0,1:T(2,128)S(1)}, u32[]{:S(2)}, u32[]{:S(2)}) %all-to-all-start) | async-done | bytes 393248 | tf_op jit(solution)/shard_map/all_to_all | solution.py:143
  (57 shorter events, 12.4 us)
Async XLA Ops:
  2.4 3.4 %copy-start.5 = (s32[2]{0:T(128)S(1)}, s32[2]{0:T(128)}, u32[]{:S(2)}) copy-start(s32[2]{0:T(128)} %param.10) | copy-start | bytes 28
  2.4 26.7 %collective-permute-start = (f32[16384]{0:T(1024)S(1)}, f32[16384]{0:T(1024)S(1)}, u32[]{:S(2)}, u32[]{:S(2)}) collective-permute-start(f32[16384]{0:T(1024)S(1)} %bitcast.74), channel_id=1, source_target_pairs={{0,16},{16,32},{32,48},{48,64},{64,80},{80,96},{96,112},{112,128},... | collective-permute-start | bytes 196616 | tf_op jit(solution)/shard_map/ppermute | solution.py:21
  5.9 0.7 copy-start.3
  5.9 0.7 copy-start.4
  7.3 63.1 %all-to-all-start.1 = ((f32[2,16,3]{2,0,1:T(2,128)}), f32[2,16,3]{2,0,1:T(2,128)S(1)}, u32[]{:S(2)}, u32[]{:S(2)}) async-start(f32[2,16,3]{2,0,1:T(2,128)} %tile.2), calls=%async_computation.1 | async-start | bytes 32768 | tf_op jit(solution)/shard_map/all_to_all | solution.py:144
  24.3 0.9 copy-start.1
  25.2 0.9 copy-start.2
  26.1 0.9 copy-start
  70.4 45.2 %all-to-all-start = ((f32[2,16,3072]{2,0,1:T(2,128)}), f32[2,16,3072]{2,0,1:T(2,128)S(1)}, u32[]{:S(2)}, u32[]{:S(2)}) async-start(f32[2,16,3072]{2,0,1:T(2,128)} %bitcast.6), calls=%async_computation | async-start | bytes 786432 | tf_op jit(solution)/shard_map/all_to_all | solution.py:143
where the time goes:
time: 118 us; the launch traced here: 117 us
  starting transfers between devices  34.7 us (29%)
  waiting for transfers between devices  29.2 us (25%)
  matrix products  22.9 us (19%)
  local copies, waits for them, and re-layouts  20.2 us (17%)
  other arithmetic  8.36 us (7%)
  between operations  1.71 us (1%)
    all_to_all x1, waiting for transfers between devices, local(): lax.all_to_all(aligned, 'bank', split_axis=1, concat_axis=0, tiled=True)  29.2 us
    all_to_all x1, starting transfers between devices, local(): lax.all_to_all(traits_rep, 'bank', split_axis=1, concat_axis=0, tiled=True)  16.9 us
    all_to_all x1, starting transfers between devices, local(): lax.all_to_all(aligned, 'bank', split_axis=1, concat_axis=0, tiled=True)  14.4 us
    gather x8, local copies, waits for them, and re-layouts  13.5 us
    dot_general x4, matrix products, contract_last(): lax.dot_general(left_mat, right_mat, (((1,), (1,)), ((), ())), precision=...  7.51 us
    unnamed x20, local copies, waits for them, and re-layouts  3.98 us
    select_n x1, other arithmetic, log_bessel(): return jnp.where(rho_val < 3.75, jnp.log(small_poly), large_val)  3.79 us
    ppermute x1, starting transfers between devices, passed_along(): return lax.ppermute(array, axis, pairs)  3.4 us
  transfers between devices with their start and end apart: 3, of which 1 were waited for; matrix products, arithmetic and copies ran while one was open for 38% of the time, Pallas kernels for 0%

commit v1 on v0

v1 whole, which is shorter than its diff:
```python
import functools
import math

import jax
import jax.numpy as jnp
import ml_dtypes
import numpy as np
from jax import lax
from jax.experimental import pallas as pl
from jax.experimental.pallas import tpu as pltpu
from jax.sharding import PartitionSpec as P

NFFT = 65536
OVER = 16384
RATE = 4096
HOP = 49152
F32, BF16 = jnp.float32, jnp.bfloat16
MESH = pl.DeviceIdType.MESH
CHUNKS = 3
GROUP = 8


def halves(table):
    high = table.astype(ml_dtypes.bfloat16)
    low = (table - high.astype(np.float64)).astype(ml_dtypes.bfloat16)
    return high, low


@functools.cache
def tables():
    turn = np.outer(np.arange(256), np.arange(256)) % 256 * (2 * np.pi / 256)
    cos, sin = np.cos(turn), np.sin(turn)
    first = np.concatenate([cos, -sin])
    high, low = halves(first)
    own = np.concatenate(
        [high[:, 64:], low[:, 64:], high[:, 64:], np.zeros_like(high[:, :64])], axis=1
    )
    halo = np.concatenate(
        [high[:, :64], low[:, :64], high[:, :64], np.zeros_like(high[:, :64])], axis=1
    )
    second = np.stack(halves(np.block([[cos[:128], sin[:128]], [-sin[:128], cos[:128]]])))
    third = np.stack(halves(np.block([[cos[:, :128], -sin[:, :128]], [sin[:, :128], cos[:, :128]]])))
    order = np.array(
        [
            48 * y + 24 * z + 12 * core + 4 * j + i
            for j in range(3)
            for y in range(4)
            for core in range(2)
            for z in range(2)
            for i in range(4)
        ]
    )
    cos_t, sin_t = cos[order], sin[order]
    fourth = np.stack(halves(np.block([[cos_t, -sin_t], [sin_t, cos_t]])))
    twist = np.outer(np.arange(256), np.arange(256)) * (2 * np.pi / NFFT)
    twist = np.stack([np.cos(twist), np.sin(twist)]).astype(np.float32)
    pick = np.zeros((512, 512), ml_dtypes.bfloat16)
    for k in range(2):
        for h in range(2):
            for a in range(128):
                pick[k * 256 + h * 128 + a, (2 * a + h) * 2 + k] = 1
    return own, halo, second, third, fourth, twist, pick


def split(value):
    high = value.astype(BF16)
    return high, (value - high.astype(F32)).astype(BF16)


def mul(left, right):
    return lax.dot_general(left, right, (((1,), (0,)), ((), ())), preferred_element_type=F32)


def mul_t(left, right):
    return lax.dot_general(left, right, (((1,), (1,)), ((), ())), preferred_element_type=F32)


def cos_sin_turn(fraction):
    half = (fraction - jnp.where(fraction >= 0.5, 1.0, 0.0)) * math.pi
    sq = half * half
    s = 1.0 / 6227020800.0
    for term in (-1.0 / 39916800.0, 1.0 / 362880.0, -1.0 / 5040.0, 1.0 / 120.0, -1.0 / 6.0, 1.0):
        s = s * sq + term
    s = s * half
    c = -1.0 / 87178291200.0
    for term in (
        1.0 / 479001600.0,
        -1.0 / 3628800.0,
        1.0 / 40320.0,
        -1.0 / 720.0,
        1.0 / 24.0,
        -0.5,
        1.0,
    ):
        c = c * sq + term
    return 1.0 - 2.0 * s * s, 2.0 * s * c


def log_bessel(power):
    edge = 3.75 * 3.75
    t = jnp.minimum(power, edge) * (1.0 / edge)
    small = jnp.full_like(t, 0.0045813)
    for term in (0.0360768, 0.2659732, 1.2067492, 3.0899424, 3.5156229, 1.0):
        small = small * t + term
    above = jnp.maximum(power, edge)
    inverse = lax.rsqrt(above)
    x = above * inverse
    q = 3.75 * inverse
    large = jnp.full_like(t, 0.00392377)
    for term in (
        -0.01647633,
        0.02635537,
        -0.02057706,
        0.00916281,
        -0.00157565,
        0.00225319,
        0.01328592,
        0.39894228,
    ):
        large = large * q + term
    is_small = power < edge
    return jnp.where(is_small, 0.0, x) + jnp.log(
        jnp.where(is_small, small, large * lax.rsqrt(x))
    )


def kernel(
    strain_hbm, asd_hbm, tmpl_hbm, own_hbm, halo_hbm, second_hbm, third_hbm, fourth_hbm, twist_hbm, pick_hbm,
    len_ref, weight_ref, mass_ref, valid_ref,
    log_ref, chirp_ref, delay_ref,
    strain, asd, tmpl, own_w, halo_w, second_w, third_w, fourth_w, twist, pick,
    gated, halo, filt, corr, send, recv, trait, traits, prior, priors, zsend, zrecv, zown,
    in_sem, halo_sem, send_sem, recv_sem, trait_send, trait_recv, prior_sem, zsend_sem, zrecv_sem,
):
    seg, bank = lax.axis_index("seg"), lax.axis_index("bank")
    seg_count = lax.axis_size("seg")
    y, z, core = bank // 4, bank // 2 % 2, bank % 2
    rank = y * 2 + core

    def bank_of(rank_, z_):
        return rank_ // 2 * 4 + z_ * 2 + rank_ % 2

    sources = (strain_hbm, asd_hbm, tmpl_hbm, pick_hbm, own_hbm, twist_hbm, halo_hbm, second_hbm, third_hbm, fourth_hbm)
    targets = (strain, asd, tmpl, pick, own_w, twist, halo_w, second_w, third_w, fourth_w)
    loads = [
        pltpu.make_async_copy(source, target, in_sem.at[i])
        for i, (source, target) in enumerate(zip(sources, targets))
    ]
    for load in loads:
        load.start()

    barrier = pltpu.get_barrier_semaphore()

    @pl.when(seg > 0)
    def _():
        pl.semaphore_signal(barrier, inc=1, device_id=(seg - 1, bank), device_id_type=MESH)

    peers = [(seg, bank_of((rank + o) % GROUP, z)) for o in range(1, GROUP)]
    opposite = (seg, bank_of(rank, 1 - z))
    for peer in peers + [opposite]:
        pl.semaphore_signal(barrier, inc=1, device_id=peer, device_id_type=MESH)

    row = lax.broadcasted_iota(jnp.int32, (8, 128), 0)
    facts = (
        weight_ref[0] + weight_ref[1],
        mass_ref[0],
        mass_ref[1],
        len_ref[0].astype(F32) * (1.0 / RATE),
        len_ref[1].astype(F32) * (1.0 / RATE),
    )
    tile = jnp.zeros((8, 128), F32)
    for i, fact in enumerate(facts):
        tile = jnp.where(row == i, fact, tile)
    trait[...] = tile

    loads[0].wait()
    for i in range(47, -1, -1):
        gated[8 * i : 8 * i + 8, :] = strain[8 * i : 8 * i + 8, :] * valid_ref[i].astype(F32)

    pl.semaphore_wait(barrier, GROUP + 1 - (seg + 1) // seg_count)

    def halo_copy():
        return pltpu.make_async_remote_copy(
            src_ref=gated.at[256:384], dst_ref=halo, send_sem=halo_sem.at[0], recv_sem=halo_sem.at[1],
            device_id=(seg + 1, bank), device_id_type=MESH,
        )

    @pl.when(seg < seg_count - 1)
    def _():
        halo_copy().start()

    @pl.when(seg == 0)
    def _():
        halo[...] = jnp.zeros((128, 128), F32)

    trait_copies = [
        pltpu.make_async_remote_copy(
            src_ref=trait, dst_ref=traits.at[o], send_sem=trait_send.at[o], recv_sem=trait_recv.at[o],
            device_id=peers[o - 1], device_id_type=MESH,
        )
        for o in range(1, GROUP)
    ]
    for copy in trait_copies:
        copy.start()

    def frame(ref, begin, count):
        return jnp.concatenate(
            [ref[pl.ds(begin, count, 2), :], ref[pl.ds(begin + 1, count, 2), :]], axis=1
        )

    high, low = split(frame(gated, 0, 192))
    loads[4].wait()
    blank = jnp.zeros((64, 256), BF16)
    part = mul(own_w[...], jnp.concatenate([high, high, low, blank], axis=0))

    loads[1].wait()
    loads[2].wait()
    loads[3].wait()
    level = frame(asd, 0, 128)
    deal = mul(pick[...], jnp.concatenate([tmpl[0], tmpl[1]], axis=1))
    for k in range(2):
        parts = [deal[256 * k + 128 * h : 256 * k + 128 * h + 128] for h in range(2)]
        tmpl_re = jnp.concatenate([p[:, :128] for p in parts], axis=1)
        tmpl_im = jnp.concatenate([p[:, 128:] for p in parts], axis=1)
        sigma = jnp.sum(level * level * (tmpl_re * tmpl_re + tmpl_im * tmpl_im), keepdims=True)
        start = OVER - len_ref[k]
        index = lax.broadcasted_iota(jnp.int32, (128, 128), 0) * start % 256
        long_cos, long_sin = cos_sin_turn(index.astype(F32) * (1.0 / 256))
        index = lax.broadcasted_iota(jnp.int32, (1, 256), 1) * start % NFFT
        short_cos, short_sin = cos_sin_turn(index.astype(F32) * (1.0 / NFFT))
        long_cos = jnp.concatenate([long_cos, long_cos], axis=1)
        long_sin = jnp.concatenate([long_sin, long_sin], axis=1)
        turn_re = long_cos * short_cos - long_sin * short_sin
        turn_im = long_cos * short_sin + long_sin * short_cos
        scale = level * (lax.rsqrt(sigma) * (1.0 / math.sqrt(NFFT)))
        filt[k, 0] = (tmpl_re * turn_re + tmpl_im * turn_im) * scale
        filt[k, 1] = (tmpl_re * turn_im - tmpl_im * turn_re) * scale

    @pl.when(seg > 0)
    def _():
        halo_copy().wait_recv()

    loads[6].wait()
    high, low = split(frame(halo, 0, 64))
    part = part + mul(halo_w[...], jnp.concatenate([high, high, low, blank], axis=0))
    loads[5].wait()
    twist_cos, twist_sin = twist[0], twist[1]
    turned = jnp.concatenate(
        [
            part[:256] * twist_cos + part[256:] * twist_sin,
            part[256:] * twist_cos - part[:256] * twist_sin,
        ],
        axis=1,
    )
    high, low = split(turned)
    loads[7].wait()
    spec = mul_t(
        jnp.concatenate([second_w[0], second_w[1], second_w[0]], axis=1),
        jnp.concatenate([high, high, low], axis=1),
    )
    spec_re, spec_im = spec[:128], spec[128:]
    prods = []
    for k in range(2):
        filt_re, filt_im = filt[k, 0], filt[k, 1]
        prods.append(
            jnp.concatenate(
                [spec_re * filt_re - spec_im * filt_im, spec_re * filt_im + spec_im * filt_re], axis=0
            )
        )
    loads[8].wait()
    loads[9].wait()
    third = jnp.concatenate([third_w[0], third_w[1], third_w[0]], axis=1)
    fourth = jnp.concatenate([fourth_w[0], fourth_w[1], fourth_w[0]], axis=1)
    for k in range(2):
        high, low = split(prods[k])
        inner = mul(third, jnp.concatenate([high, high, low], axis=0))
        turned = jnp.concatenate(
            [
                inner[:256] * twist_cos - inner[256:] * twist_sin,
                inner[:256] * twist_sin + inner[256:] * twist_cos,
            ],
            axis=1,
        )
        high, low = split(turned)
        corr[k] = mul_t(fourth, jnp.concatenate([high, high, low], axis=1))

    def score_copy(j, o):
        return pltpu.make_async_remote_copy(
            src_ref=send.at[j, (rank + o) % GROUP], dst_ref=recv.at[j, o],
            send_sem=send_sem.at[j, o], recv_sem=recv_sem.at[j, o],
            device_id=(seg, bank_of((rank + o) % GROUP, z)), device_id_type=MESH,
        )

    log_weight = [jnp.log(jnp.full((8, 256), weight_ref[k], F32)) for k in range(2)]
    for j in range(CHUNKS):
        for o in (4, 5, 3, 2, 6, 7, 1, 0):
            dest = (rank + o) % GROUP
            begin = pl.multiple_of(j * 64 + dest * 8, 8)
            for k in range(2):
                re = corr[k, pl.ds(begin, 8), :]
                im = corr[k, pl.ds(begin + 192, 8), :]
                send[j, dest, k] = log_bessel(re * re + im * im) + log_weight[k]
            if o:
                score_copy(j, o).start()

    for copy in trait_copies:
        copy.wait_recv()
    traits[0] = trait[...]
    weight_sum = traits[0, 0:1, :]
    for o in range(1, GROUP):
        weight_sum = weight_sum + traits[o, 0:1, :]
    prior[...] = jnp.broadcast_to(weight_sum, (8, 128))
    prior_copy = pltpu.make_async_remote_copy(
        src_ref=prior, dst_ref=priors, send_sem=prior_sem.at[0], recv_sem=prior_sem.at[1],
        device_id=opposite, device_id_type=MESH,
    )
    prior_copy.start()

    def z_copy(j):
        return pltpu.make_async_remote_copy(
            src_ref=zsend.at[j], dst_ref=zrecv.at[j], send_sem=zsend_sem.at[j], recv_sem=zrecv_sem.at[j],
            device_id=opposite, device_id_type=MESH,
        )

    for j in range(CHUNKS):
        for o in range(1, GROUP):
            score_copy(j, o).wait_recv()
        scores = [send[j, rank, k] for k in range(2)]
        for o in range(1, GROUP):
            scores += [recv[j, o, k] for k in range(2)]
        peak = functools.reduce(jnp.maximum, scores)
        total = chirp_sum = delay_sum = jnp.zeros((8, 256), F32)
        for i, score in enumerate(scores):
            o, k = divmod(i, 2)
            mass = jnp.exp(score - peak)
            total = total + mass
            chirp_sum = chirp_sum + mass * traits[o, 1 + k : 2 + k, 0:1]
            delay_sum = delay_sum + mass * traits[o, 3 + k : 4 + k, 0:1]
        inverse = 1.0 / total
        for i, value in enumerate((peak + jnp.log(total), chirp_sum * inverse, delay_sum * inverse)):
            rows = [
                jnp.concatenate([value[4 * h : 4 * h + 4, :128], value[4 * h : 4 * h + 4, 128:]], axis=0)
                for h in range(2)
            ]
            zown[j, 8 * i : 8 * i + 8] = jnp.where(z == 0, rows[0], rows[1])
            zsend[j, 8 * i : 8 * i + 8] = jnp.where(z == 0, rows[1], rows[0])
        z_copy(j).start()

    prior_copy.wait_recv()
    log_prior = jnp.log(prior[...] + priors[...])
    for j in range(CHUNKS):
        z_copy(j).wait_recv()
        mine, other = zown[j], zrecv[j]
        peak = jnp.maximum(mine[:8], other[:8])
        mass_a, mass_b = jnp.exp(mine[:8] - peak), jnp.exp(other[:8] - peak)
        total = mass_a + mass_b
        inverse = 1.0 / total
        values = (
            peak + jnp.log(total) - log_prior,
            (mass_a * mine[8:16] + mass_b * other[8:16]) * inverse,
            (mass_a * mine[16:] + mass_b * other[16:]) * inverse,
        )
        for out, value in zip((log_ref, chirp_ref, delay_ref), values):
            for h in range(2):
                out[pl.ds(8 * j + h, 4, 2), :] = value[4 * h : 4 * h + 4]

    @pl.when(seg < seg_count - 1)
    def _():
        halo_copy().wait_send()

    for copy in trait_copies + [prior_copy]:
        copy.wait_send()
    for j in range(CHUNKS):
        for o in range(1, GROUP):
            score_copy(j, o).wait_send()
        z_copy(j).wait_send()


def local(strain, inv_asd, templates, tmpl_len, weights, chirp_mass, valid):
    own, halo, second, third, fourth, twist, pick = tables()
    dealt = templates.reshape(2, 2, 256, 128).transpose(0, 2, 1, 3).reshape(2, 512, 128)
    anywhere = pl.BlockSpec(memory_space=pl.ANY)
    scalars = pl.BlockSpec(memory_space=pltpu.SMEM)
    held = pl.BlockSpec(memory_space=pltpu.VMEM)
    dma = pltpu.SemaphoreType.DMA
    share = jax.ShapeDtypeStruct((24, 128), F32)
    outs = pl.pallas_call(
        kernel,
        out_shape=(share, share, share),
        in_specs=[anywhere] * 10 + [scalars] * 4,
        out_specs=(held, held, held),
        scratch_shapes=[
            pltpu.VMEM((384, 128), F32),
            pltpu.VMEM((256, 128), F32),
            pltpu.VMEM((2, 512, 128), BF16),
            pltpu.VMEM(own.shape, BF16),
            pltpu.VMEM(halo.shape, BF16),
            pltpu.VMEM(second.shape, BF16),
            pltpu.VMEM(third.shape, BF16),
            pltpu.VMEM(fourth.shape, BF16),
            pltpu.VMEM(twist.shape, F32),
            pltpu.VMEM(pick.shape, BF16),
            pltpu.VMEM((384, 128), F32),
            pltpu.VMEM((128, 128), F32),
            pltpu.VMEM((2, 2, 128, 256), F32),
            pltpu.VMEM((2, 384, 256), F32),
            pltpu.VMEM((CHUNKS, GROUP, 2, 8, 256), F32),
            pltpu.VMEM((CHUNKS, GROUP, 2, 8, 256), F32),
            pltpu.VMEM((8, 128), F32),
            pltpu.VMEM((GROUP, 8, 128), F32),
            pltpu.VMEM((8, 128), F32),
            pltpu.VMEM((8, 128), F32),
            pltpu.VMEM((CHUNKS, 24, 128), F32),
            pltpu.VMEM((CHUNKS, 24, 128), F32),
            pltpu.VMEM((CHUNKS, 24, 128), F32),
            dma((10,)),
            dma((2,)),
            dma((CHUNKS, GROUP)),
            dma((CHUNKS, GROUP)),
            dma((GROUP,)),
            dma((GROUP,)),
            dma((2,)),
            dma((CHUNKS,)),
            dma((CHUNKS,)),
        ],
        compiler_params=pltpu.CompilerParams(
            collective_id=0, has_side_effects=True, vmem_limit_bytes=60 * 1024 * 1024
        ),
    )(
        strain.reshape(384, 128), inv_asd.reshape(256, 128), dealt,
        own, halo, second, third, fourth, twist, pick,
        tmpl_len, weights, chirp_mass, valid,
    )
    return tuple(out.reshape(3072) for out in outs)


def solution(mesh):
    placed = (P("seg"), P(), P(None, "bank", None), P("bank"), P("bank"), P("bank"), P("seg"))
    return jax.shard_map(
        local,
        mesh=mesh,
        in_specs=placed,
        out_specs=(P(("seg", "bank")), P(("seg", "bank")), P(("seg", "bank"))),
        check_vma=False,
    )
```

time: 118 us -> 39.7 us (0.34)
  the two profiles are of different devices: /device:TPU:34 before, /device:TPU:32 now
where the time goes in v1:
time: 39.7 us; the launch traced here: 39.4 us
  Pallas kernels  36.2 us (91%)
  local copies, waits for them, and re-layouts  2.63 us (7%)
  between operations  0.65 us (2%)
    pallas_call x1, Pallas kernels, local(): pl.pallas_call(kernel, out_shape=(share, share, share), in_specs=[anywher...  36.2 us
    unnamed x7, local copies, waits for them, and re-layouts  2.63 us

profile of v1, /device:TPU:32, one launch (start us, length us, event | category | flops | bytes accessed | tf_op | source)
XLA Modules:
  0.0 39.4 jit_solution(11559004344485523363)
XLA Ops:
  0.6 36.2 %shard_map.157 = (f32[24,128]{1,0:T(8,128)}, f32[24,128]{1,0:T(8,128)}, f32[24,128]{1,0:T(8,128)}) custom-call(f32[384,128]{1,0:T(8,128)} %bitcast.11, f32[256,128]{1,0:T(8,128)} %bitcast.12, bf16[2,512,128]{2,1,0:T(8,128)(2,1)} %bitcast.10, bf16[512,640]{1,0:T(8,128)(2,1)} %constant.14.clone.own_hbm, bf16[512,256]{1,0:T(8,128)(2,1)} %constant.15.clone.halo_hbm, ...), custom_call_target="tpu_custom_call" | custom-call | tf_op jit(solution)/shard_map/pallas_call | solution.py:387
  36.8 0.0 copy-start.1
  36.8 1.3 %copy.21 = f32[3072]{0:T(1024)} copy(f32[3072]{0:T(1024)} %bitcast.15) | data formatting | bytes 24576
  38.1 0.0 copy-done.1
  38.1 0.0 copy-start
  38.1 0.6 %copy.22 = f32[3072]{0:T(1024)} copy(f32[3072]{0:T(1024)S(1)} %bitcast.14) | data formatting | bytes 24576
  38.7 0.1 copy-done
  38.8 0.6 %copy.23 = f32[3072]{0:T(1024)} copy(f32[3072]{0:T(1024)S(1)} %bitcast.13) | data formatting | bytes 24576
Async XLA Ops:
  36.8 1.3 %copy-start.1 = (f32[24,128]{1,0:T(8,128)S(1)}, f32[24,128]{1,0:T(8,128)}, u32[]{:S(2)}) copy-start(f32[24,128]{1,0:T(8,128)} %get-tuple-element.7) | copy-start | bytes 36868
  38.1 0.7 %copy-start = (f32[24,128]{1,0:T(8,128)S(1)}, f32[24,128]{1,0:T(8,128)}, u32[]{:S(2)}) copy-start(f32[24,128]{1,0:T(8,128)} %get-tuple-element.8) | copy-start | bytes 36868

commit v2 on v1

--- a/solution.py
+++ b/solution.py
@@ -29,17 +29,7 @@
 @functools.cache
 def tables():
     turn = np.outer(np.arange(256), np.arange(256)) % 256 * (2 * np.pi / 256)
-    cos, sin = np.cos(turn), np.sin(turn)
-    first = np.concatenate([cos, -sin])
-    high, low = halves(first)
-    own = np.concatenate(
-        [high[:, 64:], low[:, 64:], high[:, 64:], np.zeros_like(high[:, :64])], axis=1
-    )
-    halo = np.concatenate(
-        [high[:, :64], low[:, :64], high[:, :64], np.zeros_like(high[:, :64])], axis=1
-    )
-    second = np.stack(halves(np.block([[cos[:128], sin[:128]], [-sin[:128], cos[:128]]])))
-    third = np.stack(halves(np.block([[cos[:, :128], -sin[:, :128]], [sin[:, :128], cos[:, :128]]])))
+    base = np.stack(halves(np.concatenate([np.cos(turn), np.sin(turn)])))
     order = np.array(
         [
             48 * y + 24 * z + 12 * core + 4 * j + i
@@ -50,16 +40,15 @@
             for i in range(4)
         ]
     )
-    cos_t, sin_t = cos[order], sin[order]
-    fourth = np.stack(halves(np.block([[cos_t, -sin_t], [sin_t, cos_t]])))
+    last = np.stack(halves(np.concatenate([np.cos(turn)[order], np.sin(turn)[order]])))
     twist = np.outer(np.arange(256), np.arange(256)) * (2 * np.pi / NFFT)
     twist = np.stack([np.cos(twist), np.sin(twist)]).astype(np.float32)
-    pick = np.zeros((512, 512), ml_dtypes.bfloat16)
+    pick = np.zeros((128, 128), ml_dtypes.bfloat16)
     for k in range(2):
         for h in range(2):
-            for a in range(128):
-                pick[k * 256 + h * 128 + a, (2 * a + h) * 2 + k] = 1
-    return own, halo, second, third, fourth, twist, pick
+            for a in range(32):
+                pick[k * 64 + h * 32 + a, (2 * a + h) * 2 + k] = 1
+    return base, last, twist, pick
 
 
 def split(value):
@@ -124,12 +113,26 @@
     )
 
 
+def frame(ref, begin, count):
+    return jnp.concatenate([ref[pl.ds(begin, count, 2), :], ref[pl.ds(begin + 1, count, 2), :]], axis=1)
+
+
+def turning(cos, sin):
+    return jnp.concatenate(
+        [jnp.concatenate([cos, -sin], axis=1), jnp.concatenate([sin, cos], axis=1)], axis=0
+    )
+
+
+def thrice(high, low):
+    return jnp.concatenate([high, low, high], axis=1)
+
+
 def kernel(
-    strain_hbm, asd_hbm, tmpl_hbm, own_hbm, halo_hbm, second_hbm, third_hbm, fourth_hbm, twist_hbm, pick_hbm,
+    len_hbm, weight_hbm, mass_hbm, valid_hbm, strain_hbm, asd_hbm, tmpl_hbm, base_hbm, last_hbm, twist_hbm, pick_hbm,
+    mine_log, mine_chirp, mine_delay, other_log, other_chirp, other_delay, log_prior,
     len_ref, weight_ref, mass_ref, valid_ref,
-    log_ref, chirp_ref, delay_ref,
-    strain, asd, tmpl, own_w, halo_w, second_w, third_w, fourth_w, twist, pick,
-    gated, halo, filt, corr, send, recv, trait, traits, prior, priors, zsend, zrecv, zown,
+    strain, asd, tmpl, base, last, twist, pick,
+    gated, halo, filt, corr, send, recv, trait, traits, prior, priors, zsend, zrecv,
     in_sem, halo_sem, send_sem, recv_sem, trait_send, trait_recv, prior_sem, zsend_sem, zrecv_sem,
 ):
     seg, bank = lax.axis_index("seg"), lax.axis_index("bank")
@@ -140,14 +143,23 @@
     def bank_of(rank_, z_):
         return rank_ // 2 * 4 + z_ * 2 + rank_ % 2
 
-    sources = (strain_hbm, asd_hbm, tmpl_hbm, pick_hbm, own_hbm, twist_hbm, halo_hbm, second_hbm, third_hbm, fourth_hbm)
-    targets = (strain, asd, tmpl, pick, own_w, twist, halo_w, second_w, third_w, fourth_w)
-    loads = [
-        pltpu.make_async_copy(source, target, in_sem.at[i])
-        for i, (source, target) in enumerate(zip(sources, targets))
-    ]
-    for load in loads:
-        load.start()
+    pairs = (
+        (valid_hbm, valid_ref),
+        (strain_hbm.at[256:384], strain.at[256:384]),
+        (strain_hbm.at[0:256], strain.at[0:256]),
+        (base_hbm, base),
+        (len_hbm, len_ref),
+        (weight_hbm, weight_ref),
+        (mass_hbm, mass_ref),
+        (pick_hbm, pick),
+        (tmpl_hbm, tmpl),
+        (asd_hbm, asd),
+        (twist_hbm, twist),
+        (last_hbm, last),
+    )
+    loads = [pltpu.make_async_copy(source, target, in_sem.at[i]) for i, (source, target) in enumerate(pairs)]
+    loads[0].start()
+    loads[1].start()
 
     barrier = pltpu.get_barrier_semaphore()
 
@@ -157,9 +169,37 @@
 
     peers = [(seg, bank_of((rank + o) % GROUP, z)) for o in range(1, GROUP)]
     opposite = (seg, bank_of(rank, 1 - z))
-    for peer in peers + [opposite]:
+    for peer in [opposite] + peers:
         pl.semaphore_signal(barrier, inc=1, device_id=peer, device_id_type=MESH)
-
+    for load in loads[2:]:
+        load.start()
+
+    def gate(begin, end):
+        for i in range(begin, end):
+            gated[8 * i : 8 * i + 8, :] = strain[8 * i : 8 * i + 8, :] * valid_ref[i].astype(F32)
+
+    loads[0].wait()
+    loads[1].wait()
+    gate(32, 48)
+
+    pl.semaphore_wait(barrier, GROUP + 1 - (seg + 1) // seg_count)
+
+    def halo_copy():
+        return pltpu.make_async_remote_copy(
+            src_ref=gated.at[256:384], dst_ref=halo, send_sem=halo_sem.at[0], recv_sem=halo_sem.at[1],
+            device_id=(seg + 1, bank), device_id_type=MESH,
+        )
+
+    @pl.when(seg < seg_count - 1)
+    def _():
+        halo_copy().start()
+
+    @pl.when(seg == 0)
+    def _():
+        halo[...] = jnp.zeros((128, 128), F32)
+
+    for i in range(4, 7):
+        loads[i].wait()
     row = lax.broadcasted_iota(jnp.int32, (8, 128), 0)
     facts = (
         weight_ref[0] + weight_ref[1],
@@ -172,27 +212,6 @@
     for i, fact in enumerate(facts):
         tile = jnp.where(row == i, fact, tile)
     trait[...] = tile
-
-    loads[0].wait()
-    for i in range(47, -1, -1):
-        gated[8 * i : 8 * i + 8, :] = strain[8 * i : 8 * i + 8, :] * valid_ref[i].astype(F32)
-
-    pl.semaphore_wait(barrier, GROUP + 1 - (seg + 1) // seg_count)
-
-    def halo_copy():
-        return pltpu.make_async_remote_copy(
-            src_ref=gated.at[256:384], dst_ref=halo, send_sem=halo_sem.at[0], recv_sem=halo_sem.at[1],
-            device_id=(seg + 1, bank), device_id_type=MESH,
-        )
-
-    @pl.when(seg < seg_count - 1)
-    def _():
-        halo_copy().start()
-
-    @pl.when(seg == 0)
-    def _():
-        halo[...] = jnp.zeros((128, 128), F32)
-
     trait_copies = [
         pltpu.make_async_remote_copy(
             src_ref=trait, dst_ref=traits.at[o], send_sem=trait_send.at[o], recv_sem=trait_recv.at[o],
@@ -203,23 +222,26 @@
     for copy in trait_copies:
         copy.start()
 
-    def frame(ref, begin, count):
-        return jnp.concatenate(
-            [ref[pl.ds(begin, count, 2), :], ref[pl.ds(begin + 1, count, 2), :]], axis=1
-        )
-
+    loads[2].wait()
+    gate(0, 32)
     high, low = split(frame(gated, 0, 192))
-    loads[4].wait()
+    loads[3].wait()
     blank = jnp.zeros((64, 256), BF16)
-    part = mul(own_w[...], jnp.concatenate([high, high, low, blank], axis=0))
-
-    loads[1].wait()
-    loads[2].wait()
-    loads[3].wait()
+    first = thrice(base[0], base[1])
+    part = mul(first, jnp.concatenate([blank, high, blank, high, blank, low], axis=0))
+
+    loads[7].wait()
+    loads[8].wait()
+    deal = []
+    for i in range(4):
+        rows = slice(128 * i, 128 * i + 128)
+        deal.append(mul(pick[...], jnp.concatenate([tmpl[0, rows], tmpl[1, rows]], axis=1)))
+    loads[9].wait()
     level = frame(asd, 0, 128)
-    deal = mul(pick[...], jnp.concatenate([tmpl[0], tmpl[1]], axis=1))
     for k in range(2):
-        parts = [deal[256 * k + 128 * h : 256 * k + 128 * h + 128] for h in range(2)]
+        parts = [
+            jnp.concatenate([d[64 * k + 32 * h : 64 * k + 32 * h + 32] for d in deal], axis=0) for h in range(2)
+        ]
         tmpl_re = jnp.concatenate([p[:, :128] for p in parts], axis=1)
         tmpl_im = jnp.concatenate([p[:, 128:] for p in parts], axis=1)
         sigma = jnp.sum(level * level * (tmpl_re * tmpl_re + tmpl_im * tmpl_im), keepdims=True)
@@ -235,44 +257,39 @@
         scale = level * (lax.rsqrt(sigma) * (1.0 / math.sqrt(NFFT)))
         filt[k, 0] = (tmpl_re * turn_re + tmpl_im * turn_im) * scale
         filt[k, 1] = (tmpl_re * turn_im - tmpl_im * turn_re) * scale
+    loads[10].wait()
+    loads[11].wait()
 
     @pl.when(seg > 0)
     def _():
         halo_copy().wait_recv()
 
-    loads[6].wait()
     high, low = split(frame(halo, 0, 64))
-    part = part + mul(halo_w[...], jnp.concatenate([high, high, low, blank], axis=0))
-    loads[5].wait()
+    part = part + mul(
+        thrice(base[0, :, 0:128], base[1, :, 0:128]),
+        jnp.concatenate([high, blank, high, blank, low, blank], axis=0),
+    )
     twist_cos, twist_sin = twist[0], twist[1]
+
     turned = jnp.concatenate(
         [
-            part[:256] * twist_cos + part[256:] * twist_sin,
-            part[256:] * twist_cos - part[:256] * twist_sin,
+            part[:256] * twist_cos - part[256:] * twist_sin,
+            part[256:] * twist_cos + part[:256] * twist_sin,
         ],
         axis=1,
     )
     high, low = split(turned)
-    loads[7].wait()
-    spec = mul_t(
-        jnp.concatenate([second_w[0], second_w[1], second_w[0]], axis=1),
-        jnp.concatenate([high, high, low], axis=1),
-    )
+    second = [turning(base[i, 0:128], base[i, 256:384]) for i in range(2)]
+    spec = mul_t(thrice(*second), jnp.concatenate([high, high, low], axis=1))
     spec_re, spec_im = spec[:128], spec[128:]
-    prods = []
+    third = thrice(*[turning(base[i, 0:256, 0:128], base[i, 256:512, 0:128]) for i in range(2)])
+    fourth = thrice(*[turning(last[i, 0:192], last[i, 192:384]) for i in range(2)])
     for k in range(2):
         filt_re, filt_im = filt[k, 0], filt[k, 1]
-        prods.append(
-            jnp.concatenate(
-                [spec_re * filt_re - spec_im * filt_im, spec_re * filt_im + spec_im * filt_re], axis=0
-            )
-        )
-    loads[8].wait()
-    loads[9].wait()
-    third = jnp.concatenate([third_w[0], third_w[1], third_w[0]], axis=1)
-    fourth = jnp.concatenate([fourth_w[0], fourth_w[1], fourth_w[0]], axis=1)
-    for k in range(2):
-        high, low = split(prods[k])
+        prod = jnp.concatenate(
+            [spec_re * filt_re + spec_im * filt_im, spec_re * filt_im - spec_im * filt_re], axis=0
+        )
+        high, low = split(prod)
         inner = mul(third, jnp.concatenate([high, high, low], axis=0))
         turned = jnp.concatenate(
             [
@@ -337,32 +354,20 @@
             chirp_sum = chirp_sum + mass * traits[o, 1 + k : 2 + k, 0:1]
             delay_sum = delay_sum + mass * traits[o, 3 + k : 4 + k, 0:1]
         inverse = 1.0 / total
-        for i, value in enumerate((peak + jnp.log(total), chirp_sum * inverse, delay_sum * inverse)):
-            rows = [
-                jnp.concatenate([value[4 * h : 4 * h + 4, :128], value[4 * h : 4 * h + 4, 128:]], axis=0)
-                for h in range(2)
-            ]
-            zown[j, 8 * i : 8 * i + 8] = jnp.where(z == 0, rows[0], rows[1])
-            zsend[j, 8 * i : 8 * i + 8] = jnp.where(z == 0, rows[1], rows[0])
+        results = (peak + jnp.log(total), chirp_sum * inverse, delay_sum * inverse)
+        for i, (value, out) in enumerate(zip(results, (mine_log, mine_chirp, mine_delay))):
+            mine = jnp.where(z == 0, value[:4], value[4:])
+            other = jnp.where(z == 0, value[4:], value[:4])
+            for h in range(2):
+                lanes = slice(128 * h, 128 * h + 128)
+                out[pl.ds(8 * j + h, 4, 2), :] = mine[:, lanes]
+                zsend[j, pl.ds(8 * i + h, 4, 2), :] = other[:, lanes]
         z_copy(j).start()
 
     prior_copy.wait_recv()
-    log_prior = jnp.log(prior[...] + priors[...])
-    for j in range(CHUNKS):
-        z_copy(j).wait_recv()
-        mine, other = zown[j], zrecv[j]
-        peak = jnp.maximum(mine[:8], other[:8])
-        mass_a, mass_b = jnp.exp(mine[:8] - peak), jnp.exp(other[:8] - peak)
-        total = mass_a + mass_b
-        inverse = 1.0 / total
-        values = (
-            peak + jnp.log(total) - log_prior,
-            (mass_a * mine[8:16] + mass_b * other[8:16]) * inverse,
-            (mass_a * mine[16:] + mass_b * other[16:]) * inverse,
-        )
-        for out, value in zip((log_ref, chirp_ref, delay_ref), values):
-            for h in range(2):
-                out[pl.ds(8 * j + h, 4, 2), :] = value[4 * h : 4 * h + 4]
+    level = jnp.log(prior[...] + priors[...])
+    for j in range(CHUNKS):
+        log_prior[8 * j : 8 * j + 8] = level
 
     @pl.when(seg < seg_count - 1)
     def _():
@@ -373,31 +378,35 @@
     for j in range(CHUNKS):
         for o in range(1, GROUP):
             score_copy(j, o).wait_send()
+    for j in range(CHUNKS):
         z_copy(j).wait_send()
+    for j in range(CHUNKS):
+        z_copy(j).wait_recv()
+        for i, out in enumerate((other_log, other_chirp, other_delay)):
+            out[8 * j : 8 * j + 8] = zrecv[j, 8 * i : 8 * i + 8]
 
 
 def local(strain, inv_asd, templates, tmpl_len, weights, chirp_mass, valid):
-    own, halo, second, third, fourth, twist, pick = tables()
+    base, last, twist, pick = tables()
     dealt = templates.reshape(2, 2, 256, 128).transpose(0, 2, 1, 3).reshape(2, 512, 128)
     anywhere = pl.BlockSpec(memory_space=pl.ANY)
-    scalars = pl.BlockSpec(memory_space=pltpu.SMEM)
     held = pl.BlockSpec(memory_space=pltpu.VMEM)
     dma = pltpu.SemaphoreType.DMA
-    share = jax.ShapeDtypeStruct((24, 128), F32)
-    outs = pl.pallas_call(
+    mine_log, mine_chirp, mine_delay, other_log, other_chirp, other_delay, log_prior = pl.pallas_call(
         kernel,
-        out_shape=(share, share, share),
-        in_specs=[anywhere] * 10 + [scalars] * 4,
-        out_specs=(held, held, held),
+        out_shape=(pltpu.VMEM((24, 128), F32),) * 7,
+        in_specs=[anywhere] * 11,
+        out_specs=(held,) * 7,
         scratch_shapes=[
+            pltpu.SMEM((2,), jnp.int32),
+            pltpu.SMEM((2,), F32),
+            pltpu.SMEM((2,), F32),
+            pltpu.SMEM((48,), jnp.int32),
             pltpu.VMEM((384, 128), F32),
             pltpu.VMEM((256, 128), F32),
             pltpu.VMEM((2, 512, 128), BF16),
-            pltpu.VMEM(own.shape, BF16),
-            pltpu.VMEM(halo.shape, BF16),
-            pltpu.VMEM(second.shape, BF16),
-            pltpu.VMEM(third.shape, BF16),
-            pltpu.VMEM(fourth.shape, BF16),
+            pltpu.VMEM(base.shape, BF16),
+            pltpu.VMEM(last.shape, BF16),
             pltpu.VMEM(twist.shape, F32),
             pltpu.VMEM(pick.shape, BF16),
             pltpu.VMEM((384, 128), F32),
@@ -412,8 +421,7 @@
             pltpu.VMEM((8, 128), F32),
             pltpu.VMEM((CHUNKS, 24, 128), F32),
             pltpu.VMEM((CHUNKS, 24, 128), F32),
-            pltpu.VMEM((CHUNKS, 24, 128), F32),
-            dma((10,)),
+            dma((12,)),
             dma((2,)),
             dma((CHUNKS, GROUP)),
             dma((CHUNKS, GROUP)),
@@ -424,12 +432,19 @@
             dma((CHUNKS,)),
         ],
         compiler_params=pltpu.CompilerParams(
-            collective_id=0, has_side_effects=True, vmem_limit_bytes=60 * 1024 * 1024
+            collective_id=0, has_side_effects=True, vmem_limit_bytes=56 * 1024 * 1024
         ),
     )(
-        strain.reshape(384, 128), inv_asd.reshape(256, 128), dealt,
-        own, halo, second, third, fourth, twist, pick,
         tmpl_len, weights, chirp_mass, valid,
+        strain.reshape(384, 128), inv_asd.reshape(256, 128), dealt, base, last, twist, pick,
+    )
+    peak = jnp.maximum(mine_log, other_log)
+    mass_a, mass_b = jnp.exp(mine_log - peak), jnp.exp(other_log - peak)
+    total = mass_a + mass_b
+    outs = (
+        peak + jnp.log(total) - log_prior,
+        (mass_a * mine_chirp + mass_b * other_chirp) / total,
+        (mass_a * mine_delay + mass_b * other_delay) / total,
     )
     return tuple(out.reshape(3072) for out in outs)
 

time: 39.7 us -> 35.6 us (0.90)
  local copies, waits for them, and re-layouts: 2.63 us -> 0 us
  Pallas kernels: 36.2 us -> 34.2 us
  other arithmetic: 0 us -> 0.63 us
    unnamed x7 -> x0, local copies, waits for them, and re-layouts: 2.63 us -> none
    pallas_call x1, Pallas kernels: 36.2 us -> 34.2 us  [local(): pl.pallas_call(kernel, out_shape=(pltpu.VMEM((24, 128), F32),) * 7, in_sp...]
    reshape x0 -> x1, other arithmetic: none -> 0.63 us  [local(): return tuple((out.reshape(3072) for out in outs))]
where the time goes in v2:
time: 35.6 us; the launch traced here: 35.5 us
  Pallas kernels  34.2 us (96%)
  between operations  0.64 us (2%)
  other arithmetic  0.63 us (2%)
    pallas_call x1, Pallas kernels, local(): pl.pallas_call(kernel, out_shape=(pltpu.VMEM((24, 128), F32),) * 7, in_sp...  34.2 us

profile of v2, /device:TPU:32, one launch (start us, length us, event | category | flops | bytes accessed | tf_op | source)
XLA Modules:
  0.0 35.5 jit_solution(13107552127083791318)
XLA Ops:
  0.6 34.2 %shard_map.130 = (f32[24,128]{1,0:T(8,128)S(1)}, f32[24,128]{1,0:T(8,128)S(1)}, f32[24,128]{1,0:T(8,128)S(1)}, f32[24,128]{1,0:T(8,128)S(1)}, f32[24,128]{1,0:T(...) custom-call(s32[2]{0:T(128)} %len_hbm.1, f32[2]{0:T(128)} %weight_hbm.1, f32[2]{0:T(128)} %mass_hbm.1, ...), custom_call_target="tpu_custom_call" | custom-call | tf_op jit(solution)/shard_map/pallas_call | solution.py:395
  34.9 0.6 %divide_bitcast_fusion = (f32[3072]{0:T(1024)}, f32[3072]{0:T(1024)}, f32[3072]{0:T(1024)}) fusion(f32[24,128]{1,0:T(8,128)S(1)} %get-tuple-element.16, f32[24,128]{1,0:T(8,128)S(1)} %get-tuple-element.15, f32[24,128]{1,0:T(8,128)S(1)} %get-tuple-element.10, f32[24,128]{1,0:T(8,128)S(1)} %get-tuple-element.11, f32[24,128]{1,0:T(8,128)S(1)} %get-tuple-element.12, ...), kind=kLoop, calls=%fused_computation | loop fusion | flops 43008 | bytes 122880 | tf_op jit(solution)/shard_map/reshape | solution.py:449

commit v3 on v2

--- a/solution.py
+++ b/solution.py
@@ -16,7 +16,7 @@
 HOP = 49152
 F32, BF16 = jnp.float32, jnp.bfloat16
 MESH = pl.DeviceIdType.MESH
-CHUNKS = 3
+HALVES = 2
 GROUP = 8
 
 
@@ -30,17 +30,14 @@
 def tables():
     turn = np.outer(np.arange(256), np.arange(256)) % 256 * (2 * np.pi / 256)
     base = np.stack(halves(np.concatenate([np.cos(turn), np.sin(turn)])))
-    order = np.array(
-        [
-            48 * y + 24 * z + 12 * core + 4 * j + i
-            for j in range(3)
-            for y in range(4)
-            for core in range(2)
-            for z in range(2)
-            for i in range(4)
-        ]
-    )
-    last = np.stack(halves(np.concatenate([np.cos(turn)[order], np.sin(turn)[order]])))
+    last = []
+    for z in range(2):
+        order = []
+        for half in (1 - z, z):
+            begins = [48 * y + 24 * half + 12 * core for y in range(4) for core in range(2)]
+            order += [t + i for t in begins for i in range(8)] + [t + i for t in begins for i in range(8, 12)]
+        last.append(halves(np.concatenate([np.cos(turn)[order], np.sin(turn)[order]])))
+    last = np.array(last)
     twist = np.outer(np.arange(256), np.arange(256)) * (2 * np.pi / NFFT)
     twist = np.stack([np.cos(twist), np.sin(twist)]).astype(np.float32)
     pick = np.zeros((128, 128), ml_dtypes.bfloat16)
@@ -127,21 +124,18 @@
     return jnp.concatenate([high, low, high], axis=1)
 
 
-def kernel(
+def prepare(
     len_hbm, weight_hbm, mass_hbm, valid_hbm, strain_hbm, asd_hbm, tmpl_hbm, base_hbm, last_hbm, twist_hbm, pick_hbm,
-    mine_log, mine_chirp, mine_delay, other_log, other_chirp, other_delay, log_prior,
-    len_ref, weight_ref, mass_ref, valid_ref,
-    strain, asd, tmpl, base, last, twist, pick,
-    gated, halo, filt, corr, send, recv, trait, traits, prior, priors, zsend, zrecv,
-    in_sem, halo_sem, send_sem, recv_sem, trait_send, trait_recv, prior_sem, zsend_sem, zrecv_sem,
+    part_out, filt, trait, base, last, twist,
+    len_ref, weight_ref, mass_ref, valid_ref, strain, asd, tmpl, pick, gated, halo, in_sem, halo_sem,
 ):
     seg, bank = lax.axis_index("seg"), lax.axis_index("bank")
     seg_count = lax.axis_size("seg")
-    y, z, core = bank // 4, bank // 2 % 2, bank % 2
-    rank = y * 2 + core
-
-    def bank_of(rank_, z_):
-        return rank_ // 2 * 4 + z_ * 2 + rank_ % 2
+    barrier = pltpu.get_barrier_semaphore()
+
+    @pl.when(seg > 0)
+    def _():
+        pl.semaphore_signal(barrier, inc=1, device_id=(seg - 1, bank), device_id_type=MESH)
 
     pairs = (
         (valid_hbm, valid_ref),
@@ -155,22 +149,11 @@
         (tmpl_hbm, tmpl),
         (asd_hbm, asd),
         (twist_hbm, twist),
-        (last_hbm, last),
+        (last_hbm.at[bank // 2 % 2], last),
     )
     loads = [pltpu.make_async_copy(source, target, in_sem.at[i]) for i, (source, target) in enumerate(pairs)]
     loads[0].start()
     loads[1].start()
-
-    barrier = pltpu.get_barrier_semaphore()
-
-    @pl.when(seg > 0)
-    def _():
-        pl.semaphore_signal(barrier, inc=1, device_id=(seg - 1, bank), device_id_type=MESH)
-
-    peers = [(seg, bank_of((rank + o) % GROUP, z)) for o in range(1, GROUP)]
-    opposite = (seg, bank_of(rank, 1 - z))
-    for peer in [opposite] + peers:
-        pl.semaphore_signal(barrier, inc=1, device_id=peer, device_id_type=MESH)
     for load in loads[2:]:
         load.start()
 
@@ -181,8 +164,6 @@
     loads[0].wait()
     loads[1].wait()
     gate(32, 48)
-
-    pl.semaphore_wait(barrier, GROUP + 1 - (seg + 1) // seg_count)
 
     def halo_copy():
         return pltpu.make_async_remote_copy(
@@ -192,6 +173,7 @@
 
     @pl.when(seg < seg_count - 1)
     def _():
+        pl.semaphore_wait(barrier, 1)
         halo_copy().start()
 
     @pl.when(seg == 0)
@@ -207,20 +189,13 @@
         mass_ref[1],
         len_ref[0].astype(F32) * (1.0 / RATE),
         len_ref[1].astype(F32) * (1.0 / RATE),
+        weight_ref[0],
+        weight_ref[1],
     )
     tile = jnp.zeros((8, 128), F32)
     for i, fact in enumerate(facts):
         tile = jnp.where(row == i, fact, tile)
     trait[...] = tile
-    trait_copies = [
-        pltpu.make_async_remote_copy(
-            src_ref=trait, dst_ref=traits.at[o], send_sem=trait_send.at[o], recv_sem=trait_recv.at[o],
-            device_id=peers[o - 1], device_id_type=MESH,
-        )
-        for o in range(1, GROUP)
-    ]
-    for copy in trait_copies:
-        copy.start()
 
     loads[2].wait()
     gate(0, 32)
@@ -265,16 +240,39 @@
         halo_copy().wait_recv()
 
     high, low = split(frame(halo, 0, 64))
-    part = part + mul(
+    part_out[...] = part + mul(
         thrice(base[0, :, 0:128], base[1, :, 0:128]),
         jnp.concatenate([high, blank, high, blank, low, blank], axis=0),
     )
+
+    @pl.when(seg < seg_count - 1)
+    def _():
+        halo_copy().wait_send()
+
+
+def match(
+    part, filt, trait, base, last, twist,
+    mine_log, mine_chirp, mine_delay, other_log, other_chirp, other_delay, log_prior,
+    send, recv, traits, packet, arrived, send_sem, recv_sem, trait_send, trait_recv, z_sem,
+):
+    seg, bank = lax.axis_index("seg"), lax.axis_index("bank")
+    y, z, core = bank // 4, bank // 2 % 2, bank % 2
+    rank = y * 2 + core
+
+    def bank_of(rank_, z_):
+        return rank_ // 2 * 4 + z_ * 2 + rank_ % 2
+
+    barrier = pltpu.get_barrier_semaphore()
+    peers = [(seg, bank_of((rank + o) % GROUP, z)) for o in range(1, GROUP)]
+    opposite = (seg, bank_of(rank, 1 - z))
+    for peer in [opposite] + peers:
+        pl.semaphore_signal(barrier, inc=1, device_id=peer, device_id_type=MESH)
     twist_cos, twist_sin = twist[0], twist[1]
 
     turned = jnp.concatenate(
         [
-            part[:256] * twist_cos - part[256:] * twist_sin,
-            part[256:] * twist_cos + part[:256] * twist_sin,
+            part[0:256] * twist_cos - part[256:512] * twist_sin,
+            part[256:512] * twist_cos + part[0:256] * twist_sin,
         ],
         axis=1,
     )
@@ -284,6 +282,7 @@
     spec_re, spec_im = spec[:128], spec[128:]
     third = thrice(*[turning(base[i, 0:256, 0:128], base[i, 256:512, 0:128]) for i in range(2)])
     fourth = thrice(*[turning(last[i, 0:192], last[i, 192:384]) for i in range(2)])
+    weights = []
     for k in range(2):
         filt_re, filt_im = filt[k, 0], filt[k, 1]
         prod = jnp.concatenate(
@@ -299,26 +298,47 @@
             axis=1,
         )
         high, low = split(turned)
-        corr[k] = mul_t(fourth, jnp.concatenate([high, high, low], axis=1))
+        weights.append(jnp.concatenate([high, high, low], axis=1))
 
     def score_copy(j, o):
         return pltpu.make_async_remote_copy(
             src_ref=send.at[j, (rank + o) % GROUP], dst_ref=recv.at[j, o],
             send_sem=send_sem.at[j, o], recv_sem=recv_sem.at[j, o],
-            device_id=(seg, bank_of((rank + o) % GROUP, z)), device_id_type=MESH,
-        )
-
-    log_weight = [jnp.log(jnp.full((8, 256), weight_ref[k], F32)) for k in range(2)]
-    for j in range(CHUNKS):
-        for o in (4, 5, 3, 2, 6, 7, 1, 0):
-            dest = (rank + o) % GROUP
-            begin = pl.multiple_of(j * 64 + dest * 8, 8)
-            for k in range(2):
-                re = corr[k, pl.ds(begin, 8), :]
-                im = corr[k, pl.ds(begin + 192, 8), :]
-                send[j, dest, k] = log_bessel(re * re + im * im) + log_weight[k]
-            if o:
-                score_copy(j, o).start()
+            device_id=peers[o - 1], device_id_type=MESH,
+        )
+
+    trait_copies = [
+        pltpu.make_async_remote_copy(
+            src_ref=trait, dst_ref=traits.at[o], send_sem=trait_send.at[o], recv_sem=trait_recv.at[o],
+            device_id=peers[o - 1], device_id_type=MESH,
+        )
+        for o in range(1, GROUP)
+    ]
+    log_weight = [jnp.log(jnp.broadcast_to(trait[5 + k : 6 + k, 0:1], (8, 256))) for k in range(2)]
+    for j in range(HALVES):
+        fourth = thrice(
+            *[turning(last[i, 96 * j : 96 * j + 96], last[i, 96 * j + 192 : 96 * j + 288]) for i in range(2)]
+        )
+        for k in range(2):
+            corr = mul_t(fourth, weights[k])
+
+            def score(p):
+                re, im = corr[p : p + 8], corr[p + 96 : p + 104]
+                return log_bessel(re * re + im * im) + log_weight[k]
+
+            for block in range(GROUP):
+                send[j, block, 8 * k : 8 * k + 8] = score(8 * block)
+            for block in range(0, GROUP, 2):
+                both = score(64 + 4 * block)
+                send[j, block, 16 + 4 * k : 20 + 4 * k] = both[:4]
+                send[j, block + 1, 16 + 4 * k : 20 + 4 * k] = both[4:]
+        if j == 0:
+            pl.semaphore_wait(barrier, GROUP)
+        for o in (4, 5, 3, 2, 6, 7, 1):
+            score_copy(j, o).start()
+        if j == 0:
+            for copy in trait_copies:
+                copy.start()
 
     for copy in trait_copies:
         copy.wait_recv()
@@ -326,64 +346,72 @@
     weight_sum = traits[0, 0:1, :]
     for o in range(1, GROUP):
         weight_sum = weight_sum + traits[o, 0:1, :]
-    prior[...] = jnp.broadcast_to(weight_sum, (8, 128))
-    prior_copy = pltpu.make_async_remote_copy(
-        src_ref=prior, dst_ref=priors, send_sem=prior_sem.at[0], recv_sem=prior_sem.at[1],
+    packet[72:80] = jnp.broadcast_to(weight_sum, (8, 128))
+
+    z_copy = pltpu.make_async_remote_copy(
+        src_ref=packet, dst_ref=arrived, send_sem=z_sem.at[0], recv_sem=z_sem.at[1],
         device_id=opposite, device_id_type=MESH,
     )
-    prior_copy.start()
-
-    def z_copy(j):
-        return pltpu.make_async_remote_copy(
-            src_ref=zsend.at[j], dst_ref=zrecv.at[j], send_sem=zsend_sem.at[j], recv_sem=zrecv_sem.at[j],
-            device_id=opposite, device_id_type=MESH,
-        )
-
-    for j in range(CHUNKS):
+    is_first = lax.broadcasted_iota(jnp.int32, (8, 256), 0) < 4
+    for j in range(HALVES):
         for o in range(1, GROUP):
             score_copy(j, o).wait_recv()
-        scores = [send[j, rank, k] for k in range(2)]
-        for o in range(1, GROUP):
-            scores += [recv[j, o, k] for k in range(2)]
+
+        def arrivals(begin):
+            return [send[j, rank, begin : begin + 8]] + [recv[j, o, begin : begin + 8] for o in range(1, GROUP)]
+
+        def fact(o, i):
+            return traits[o, i : i + 1, 0:1]
+
+        scores = [arrivals(0), arrivals(8)]
+        peak = functools.reduce(jnp.maximum, scores[0] + scores[1])
+        total = chirp_sum = delay_sum = jnp.zeros((8, 256), F32)
+        for o in range(GROUP):
+            for k in range(2):
+                mass = jnp.exp(scores[k][o] - peak)
+                total = total + mass
+                chirp_sum = chirp_sum + mass * fact(o, 1 + k)
+                delay_sum = delay_sum + mass * fact(o, 3 + k)
+        inverse = 1.0 / total
+        upper = (peak + jnp.log(total), chirp_sum * inverse, delay_sum * inverse)
+
+        scores = arrivals(16)
         peak = functools.reduce(jnp.maximum, scores)
+        peak = jnp.maximum(peak[:4], peak[4:])
+        peak_twice = jnp.concatenate([peak, peak], axis=0)
         total = chirp_sum = delay_sum = jnp.zeros((8, 256), F32)
-        for i, score in enumerate(scores):
-            o, k = divmod(i, 2)
-            mass = jnp.exp(score - peak)
+        for o in range(GROUP):
+            mass = jnp.exp(scores[o] - peak_twice)
             total = total + mass
-            chirp_sum = chirp_sum + mass * traits[o, 1 + k : 2 + k, 0:1]
-            delay_sum = delay_sum + mass * traits[o, 3 + k : 4 + k, 0:1]
+            chirp_sum = chirp_sum + mass * jnp.where(is_first, fact(o, 1), fact(o, 2))
+            delay_sum = delay_sum + mass * jnp.where(is_first, fact(o, 3), fact(o, 4))
+        total, chirp_sum, delay_sum = [v[:4] + v[4:] for v in (total, chirp_sum, delay_sum)]
         inverse = 1.0 / total
-        results = (peak + jnp.log(total), chirp_sum * inverse, delay_sum * inverse)
-        for i, (value, out) in enumerate(zip(results, (mine_log, mine_chirp, mine_delay))):
-            mine = jnp.where(z == 0, value[:4], value[4:])
-            other = jnp.where(z == 0, value[4:], value[:4])
+        lower = (peak + jnp.log(total), chirp_sum * inverse, delay_sum * inverse)
+
+        for i, out in enumerate((mine_log, mine_chirp, mine_delay)):
             for h in range(2):
                 lanes = slice(128 * h, 128 * h + 128)
-                out[pl.ds(8 * j + h, 4, 2), :] = mine[:, lanes]
-                zsend[j, pl.ds(8 * i + h, 4, 2), :] = other[:, lanes]
-        z_copy(j).start()
-
-    prior_copy.wait_recv()
-    level = jnp.log(prior[...] + priors[...])
-    for j in range(CHUNKS):
-        log_prior[8 * j : 8 * j + 8] = level
-
-    @pl.when(seg < seg_count - 1)
-    def _():
-        halo_copy().wait_send()
-
-    for copy in trait_copies + [prior_copy]:
+                if j == 0:
+                    packet[pl.ds(24 * i + h, 8, 2), :] = upper[i][:, lanes]
+                    packet[pl.ds(24 * i + 16 + h, 4, 2), :] = lower[i][:, lanes]
+                else:
+                    out[pl.ds(h, 8, 2), :] = upper[i][:, lanes]
+                    out[pl.ds(16 + h, 4, 2), :] = lower[i][:, lanes]
+        if j == 0:
+            z_copy.start()
+
+    for copy in trait_copies:
         copy.wait_send()
-    for j in range(CHUNKS):
+    for j in range(HALVES):
         for o in range(1, GROUP):
             score_copy(j, o).wait_send()
-    for j in range(CHUNKS):
-        z_copy(j).wait_send()
-    for j in range(CHUNKS):
-        z_copy(j).wait_recv()
-        for i, out in enumerate((other_log, other_chirp, other_delay)):
-            out[8 * j : 8 * j + 8] = zrecv[j, 8 * i : 8 * i + 8]
+    z_copy.wait()
+    for i, out in enumerate((other_log, other_chirp, other_delay)):
+        out[...] = arrived[24 * i : 24 * i + 24]
+    level = jnp.log(packet[72:80] + arrived[72:80])
+    for i in range(3):
+        log_prior[8 * i : 8 * i + 8] = level
 
 
 def local(strain, inv_asd, templates, tmpl_len, weights, chirp_mass, valid):
@@ -392,11 +420,18 @@
     anywhere = pl.BlockSpec(memory_space=pl.ANY)
     held = pl.BlockSpec(memory_space=pltpu.VMEM)
     dma = pltpu.SemaphoreType.DMA
-    mine_log, mine_chirp, mine_delay, other_log, other_chirp, other_delay, log_prior = pl.pallas_call(
-        kernel,
-        out_shape=(pltpu.VMEM((24, 128), F32),) * 7,
+    ready = pl.pallas_call(
+        prepare,
+        out_shape=(
+            pltpu.VMEM((512, 256), F32),
+            pltpu.VMEM((2, 2, 128, 256), F32),
+            pltpu.VMEM((8, 128), F32),
+            pltpu.VMEM(base.shape, BF16),
+            pltpu.VMEM(last.shape[1:], BF16),
+            pltpu.VMEM(twist.shape, F32),
+        ),
         in_specs=[anywhere] * 11,
-        out_specs=(held,) * 7,
+        out_specs=(held,) * 6,
         scratch_shapes=[
             pltpu.SMEM((2,), jnp.int32),
             pltpu.SMEM((2,), F32),
@@ -405,31 +440,11 @@
             pltpu.VMEM((384, 128), F32),
             pltpu.VMEM((256, 128), F32),
             pltpu.VMEM((2, 512, 128), BF16),
-            pltpu.VMEM(base.shape, BF16),
-            pltpu.VMEM(last.shape, BF16),
-            pltpu.VMEM(twist.shape, F32),
             pltpu.VMEM(pick.shape, BF16),
             pltpu.VMEM((384, 128), F32),
             pltpu.VMEM((128, 128), F32),
-            pltpu.VMEM((2, 2, 128, 256), F32),
-            pltpu.VMEM((2, 384, 256), F32),
-            pltpu.VMEM((CHUNKS, GROUP, 2, 8, 256), F32),
-            pltpu.VMEM((CHUNKS, GROUP, 2, 8, 256), F32),
-            pltpu.VMEM((8, 128), F32),
-            pltpu.VMEM((GROUP, 8, 128), F32),
-            pltpu.VMEM((8, 128), F32),
-            pltpu.VMEM((8, 128), F32),
-            pltpu.VMEM((CHUNKS, 24, 128), F32),
-            pltpu.VMEM((CHUNKS, 24, 128), F32),
             dma((12,)),
             dma((2,)),
-            dma((CHUNKS, GROUP)),
-            dma((CHUNKS, GROUP)),
-            dma((GROUP,)),
-            dma((GROUP,)),
-            dma((2,)),
-            dma((CHUNKS,)),
-            dma((CHUNKS,)),
         ],
         compiler_params=pltpu.CompilerParams(
             collective_id=0, has_side_effects=True, vmem_limit_bytes=56 * 1024 * 1024
@@ -438,6 +453,27 @@
         tmpl_len, weights, chirp_mass, valid,
         strain.reshape(384, 128), inv_asd.reshape(256, 128), dealt, base, last, twist, pick,
     )
+    mine_log, mine_chirp, mine_delay, other_log, other_chirp, other_delay, log_prior = pl.pallas_call(
+        match,
+        out_shape=(pltpu.VMEM((24, 128), F32),) * 7,
+        in_specs=[held] * 6,
+        out_specs=(held,) * 7,
+        scratch_shapes=[
+            pltpu.VMEM((HALVES, GROUP, 24, 256), F32),
+            pltpu.VMEM((HALVES, GROUP, 24, 256), F32),
+            pltpu.VMEM((GROUP, 8, 128), F32),
+            pltpu.VMEM((80, 128), F32),
+            pltpu.VMEM((80, 128), F32),
+            dma((HALVES, GROUP)),
+            dma((HALVES, GROUP)),
+            dma((GROUP,)),
+            dma((GROUP,)),
+            dma((2,)),
+        ],
+        compiler_params=pltpu.CompilerParams(
+            collective_id=1, has_side_effects=True, vmem_limit_bytes=56 * 1024 * 1024
+        ),
+    )(*[pltpu.with_memory_space_constraint(array, pltpu.VMEM) for array in ready])
     peak = jnp.maximum(mine_log, other_log)
     mass_a, mass_b = jnp.exp(mine_log - peak), jnp.exp(other_log - peak)
     total = mass_a + mass_b

time: 35.6 us -> 35 us (0.983)
  Pallas kernels: 34.2 us -> 33.5 us
    pallas_call x1 -> x2, Pallas kernels: 34.2 us -> 33.5 us  [the longest x1 25.8 us: local(): pl.pallas_call(match, out_shape=(pltpu.VMEM((24, 128), F32),) * 7, in_spe...]
where the time goes in v3:
time: 35 us; the launch traced here: 34.8 us
  Pallas kernels  33.5 us (96%)
  between operations  0.65 us (2%)
  other arithmetic  0.63 us (2%)
    pallas_call x1, Pallas kernels, local(): pl.pallas_call(match, out_shape=(pltpu.VMEM((24, 128), F32),) * 7, in_spe...  25.8 us
    pallas_call x1, Pallas kernels, local(): pl.pallas_call(prepare, out_shape=(pltpu.VMEM((512, 256), F32), pltpu.VME...  7.72 us

profile of v3, /device:TPU:32, one launch (start us, length us, event | category | flops | bytes accessed | tf_op | source)
XLA Modules:
  0.0 34.8 jit_solution(14248127507812108266)
XLA Ops:
  0.6 7.7 %shard_map.130 = (f32[512,256]{1,0:T(8,128)S(1)}, f32[2,2,128,256]{3,2,1,0:T(8,128)S(1)}, f32[8,128]{1,0:T(8,128)S(1)}, bf16[2,512,256]{2,1,0:T(8,128)(2,1)S(1)}...) custom-call(s32[2]{0:T(128)} %len_hbm.1, f32[2]{0:T(128)} %weight_hbm.1, f32[2]{0:T(128)} %mass_hbm.1, ...), custom_call_target="tpu_custom_call" | custom-call | tf_op jit(solution)/shard_map/pallas_call | solution.py:423
  8.4 25.8 %shard_map.131 = (f32[24,128]{1,0:T(8,128)S(1)}, f32[24,128]{1,0:T(8,128)S(1)}, f32[24,128]{1,0:T(8,128)S(1)}, f32[24,128]{1,0:T(8,128)S(1)}, f32[24,128]{1,0:T(...) custom-call(f32[512,256]{1,0:T(8,128)S(1)} %get-tuple-element.16.part, ...), custom_call_target="tpu_custom_call" | custom-call | tf_op jit(solution)/shard_map/pallas_call | solution.py:456
  34.2 0.6 %divide_bitcast_fusion = (f32[3072]{0:T(1024)}, f32[3072]{0:T(1024)}, f32[3072]{0:T(1024)}) fusion(f32[24,128]{1,0:T(8,128)S(1)} %get-tuple-element.28, f32[24,128]{1,0:T(8,128)S(1)} %get-tuple-element.27, f32[24,128]{1,0:T(8,128)S(1)} %get-tuple-element.22, f32[24,128]{1,0:T(8,128)S(1)} %get-tuple-element.23, f32[24,128]{1,0:T(8,128)S(1)} %get-tuple-element.24, ...), kind=kLoop, calls=%fused_computation | loop fusion | flops 43008 | bytes 122880 | tf_op jit(solution)/shard_map/reshape | solution.py:485

commit v4 on v3

--- a/solution.py
+++ b/solution.py
@@ -278,7 +278,8 @@
     )
     high, low = split(turned)
     second = [turning(base[i, 0:128], base[i, 256:384]) for i in range(2)]
-    spec = mul_t(thrice(*second), jnp.concatenate([high, high, low], axis=1))
+    spec = mul_t(jnp.concatenate(second, axis=0), high)
+    spec = spec[:256] + spec[256:] + mul_t(second[0], low)
     spec_re, spec_im = spec[:128], spec[128:]
     third = thrice(*[turning(base[i, 0:256, 0:128], base[i, 256:512, 0:128]) for i in range(2)])
     fourth = thrice(*[turning(last[i, 0:192], last[i, 192:384]) for i in range(2)])
@@ -298,7 +299,7 @@
             axis=1,
         )
         high, low = split(turned)
-        weights.append(jnp.concatenate([high, high, low], axis=1))
+        weights.append((high, low))
 
     def score_copy(j, o):
         return pltpu.make_async_remote_copy(
@@ -316,11 +317,12 @@
     ]
     log_weight = [jnp.log(jnp.broadcast_to(trait[5 + k : 6 + k, 0:1], (8, 256))) for k in range(2)]
     for j in range(HALVES):
-        fourth = thrice(
-            *[turning(last[i, 96 * j : 96 * j + 96], last[i, 96 * j + 192 : 96 * j + 288]) for i in range(2)]
-        )
+        fourth = [turning(last[i, 96 * j : 96 * j + 96], last[i, 96 * j + 192 : 96 * j + 288]) for i in range(2)]
+        stacked = jnp.concatenate(fourth, axis=0)
         for k in range(2):
-            corr = mul_t(fourth, weights[k])
+            high, low = weights[k]
+            corr = mul_t(stacked, high)
+            corr = corr[:192] + corr[192:] + mul_t(fourth[0], low)
 
             def score(p):
                 re, im = corr[p : p + 8], corr[p + 96 : p + 104]
@@ -334,11 +336,10 @@
                 send[j, block + 1, 16 + 4 * k : 20 + 4 * k] = both[4:]
         if j == 0:
             pl.semaphore_wait(barrier, GROUP)
-        for o in (4, 5, 3, 2, 6, 7, 1):
-            score_copy(j, o).start()
-        if j == 0:
             for copy in trait_copies:
                 copy.start()
+            for o in (4, 5, 3, 2, 6, 7, 1):
+                score_copy(0, o).start()
 
     for copy in trait_copies:
         copy.wait_recv()
@@ -356,6 +357,9 @@
     for j in range(HALVES):
         for o in range(1, GROUP):
             score_copy(j, o).wait_recv()
+        if j == 0:
+            for o in (4, 5, 3, 2, 6, 7, 1):
+                score_copy(1, o).start()
 
         def arrivals(begin):
             return [send[j, rank, begin : begin + 8]] + [recv[j, o, begin : begin + 8] for o in range(1, GROUP)]

time: 35 us -> 33.8 us (0.966)
  Pallas kernels: 33.5 us -> 32.3 us
    pallas_call x1, Pallas kernels: 25.8 us -> 24.6 us  [local(): pl.pallas_call(match, out_shape=(pltpu.VMEM((24, 128), F32),) * 7, in_spe...]
where the time goes in v4:
time: 33.8 us; the launch traced here: 33.6 us
  Pallas kernels  32.3 us (96%)
  between operations  0.65 us (2%)
  other arithmetic  0.63 us (2%)
    pallas_call x1, Pallas kernels, local(): pl.pallas_call(match, out_shape=(pltpu.VMEM((24, 128), F32),) * 7, in_spe...  24.6 us
    pallas_call x1, Pallas kernels, local(): pl.pallas_call(prepare, out_shape=(pltpu.VMEM((512, 256), F32), pltpu.VME...  7.72 us

profile of v4, /device:TPU:32, one launch (start us, length us, event | category | flops | bytes accessed | tf_op | source)
XLA Modules:
  0.0 33.6 jit_solution(1055544475711557866)
XLA Ops:
  0.6 7.7 %shard_map.130 = (f32[512,256]{1,0:T(8,128)S(1)}, f32[2,2,128,256]{3,2,1,0:T(8,128)S(1)}, f32[8,128]{1,0:T(8,128)S(1)}, bf16[2,512,256]{2,1,0:T(8,128)(2,1)S(1)}...) custom-call(s32[2]{0:T(128)} %len_hbm.1, f32[2]{0:T(128)} %weight_hbm.1, f32[2]{0:T(128)} %mass_hbm.1, ...), custom_call_target="tpu_custom_call" | custom-call | tf_op jit(solution)/shard_map/pallas_call | solution.py:427
  8.4 24.6 %shard_map.131 = (f32[24,128]{1,0:T(8,128)S(1)}, f32[24,128]{1,0:T(8,128)S(1)}, f32[24,128]{1,0:T(8,128)S(1)}, f32[24,128]{1,0:T(8,128)S(1)}, f32[24,128]{1,0:T(...) custom-call(f32[512,256]{1,0:T(8,128)S(1)} %get-tuple-element.16.part, ...), custom_call_target="tpu_custom_call" | custom-call | tf_op jit(solution)/shard_map/pallas_call | solution.py:460
  33.0 0.6 %divide_bitcast_fusion = (f32[3072]{0:T(1024)}, f32[3072]{0:T(1024)}, f32[3072]{0:T(1024)}) fusion(f32[24,128]{1,0:T(8,128)S(1)} %get-tuple-element.28, f32[24,128]{1,0:T(8,128)S(1)} %get-tuple-element.27, f32[24,128]{1,0:T(8,128)S(1)} %get-tuple-element.22, f32[24,128]{1,0:T(8,128)S(1)} %get-tuple-element.23, f32[24,128]{1,0:T(8,128)S(1)} %get-tuple-element.24, ...), kind=kLoop, calls=%fused_computation | loop fusion | flops 43008 | bytes 122880 | tf_op jit(solution)/shard_map/reshape | solution.py:489

commit v5 on v4

--- a/solution.py
+++ b/solution.py
@@ -182,7 +182,7 @@
 
     for i in range(4, 7):
         loads[i].wait()
-    row = lax.broadcasted_iota(jnp.int32, (8, 128), 0)
+    lane = lax.broadcasted_iota(jnp.int32, (1, 128), 1)
     facts = (
         weight_ref[0] + weight_ref[1],
         mass_ref[0],
@@ -192,9 +192,9 @@
         weight_ref[0],
         weight_ref[1],
     )
-    tile = jnp.zeros((8, 128), F32)
+    tile = jnp.zeros((1, 128), F32)
     for i, fact in enumerate(facts):
-        tile = jnp.where(row == i, fact, tile)
+        tile = jnp.where(lane == i, fact, tile)
     trait[...] = tile
 
     loads[2].wait()
@@ -265,7 +265,7 @@
     barrier = pltpu.get_barrier_semaphore()
     peers = [(seg, bank_of((rank + o) % GROUP, z)) for o in range(1, GROUP)]
     opposite = (seg, bank_of(rank, 1 - z))
-    for peer in [opposite] + peers:
+    for peer in [peers[o - 1] for o in (4, 5, 3, 2, 6, 7, 1)] + [opposite]:
         pl.semaphore_signal(barrier, inc=1, device_id=peer, device_id_type=MESH)
     twist_cos, twist_sin = twist[0], twist[1]
 
@@ -282,7 +282,6 @@
     spec = spec[:256] + spec[256:] + mul_t(second[0], low)
     spec_re, spec_im = spec[:128], spec[128:]
     third = thrice(*[turning(base[i, 0:256, 0:128], base[i, 256:512, 0:128]) for i in range(2)])
-    fourth = thrice(*[turning(last[i, 0:192], last[i, 192:384]) for i in range(2)])
     weights = []
     for k in range(2):
         filt_re, filt_im = filt[k, 0], filt[k, 1]
@@ -301,10 +300,12 @@
         high, low = split(turned)
         weights.append((high, low))
 
-    def score_copy(j, o):
+    def score_copy(piece, o):
+        rows = ((0, slice(0, 16)), (0, slice(16, 24)), (1, slice(0, 24)))[piece]
+        j, part_of = rows
         return pltpu.make_async_remote_copy(
-            src_ref=send.at[j, (rank + o) % GROUP], dst_ref=recv.at[j, o],
-            send_sem=send_sem.at[j, o], recv_sem=recv_sem.at[j, o],
+            src_ref=send.at[j, (rank + o) % GROUP, part_of], dst_ref=recv.at[j, o, part_of],
+            send_sem=send_sem.at[piece, o], recv_sem=recv_sem.at[piece, o],
             device_id=peers[o - 1], device_id_type=MESH,
         )
 
@@ -315,7 +316,7 @@
         )
         for o in range(1, GROUP)
     ]
-    log_weight = [jnp.log(jnp.broadcast_to(trait[5 + k : 6 + k, 0:1], (8, 256))) for k in range(2)]
+    log_weight = [jnp.log(jnp.broadcast_to(trait[0:1, 5 + k : 6 + k], (8, 256))) for k in range(2)]
     for j in range(HALVES):
         fourth = [turning(last[i, 96 * j : 96 * j + 96], last[i, 96 * j + 192 : 96 * j + 288]) for i in range(2)]
         stacked = jnp.concatenate(fourth, axis=0)
@@ -336,38 +337,28 @@
                 send[j, block + 1, 16 + 4 * k : 20 + 4 * k] = both[4:]
         if j == 0:
             pl.semaphore_wait(barrier, GROUP)
+            for o in (4, 5, 3, 2, 6, 7, 1):
+                score_copy(0, o).start()
             for copy in trait_copies:
                 copy.start()
             for o in (4, 5, 3, 2, 6, 7, 1):
-                score_copy(0, o).start()
-
-    for copy in trait_copies:
-        copy.wait_recv()
-    traits[0] = trait[...]
-    weight_sum = traits[0, 0:1, :]
-    for o in range(1, GROUP):
-        weight_sum = weight_sum + traits[o, 0:1, :]
-    packet[72:80] = jnp.broadcast_to(weight_sum, (8, 128))
-
-    z_copy = pltpu.make_async_remote_copy(
-        src_ref=packet, dst_ref=arrived, send_sem=z_sem.at[0], recv_sem=z_sem.at[1],
-        device_id=opposite, device_id_type=MESH,
-    )
-    is_first = lax.broadcasted_iota(jnp.int32, (8, 256), 0) < 4
-    for j in range(HALVES):
-        for o in range(1, GROUP):
-            score_copy(j, o).wait_recv()
-        if j == 0:
-            for o in (4, 5, 3, 2, 6, 7, 1):
                 score_copy(1, o).start()
 
-        def arrivals(begin):
-            return [send[j, rank, begin : begin + 8]] + [recv[j, o, begin : begin + 8] for o in range(1, GROUP)]
-
-        def fact(o, i):
-            return traits[o, i : i + 1, 0:1]
-
-        scores = [arrivals(0), arrivals(8)]
+    def z_copy(i):
+        rows = (slice(0, 48), slice(48, 80))[i]
+        return pltpu.make_async_remote_copy(
+            src_ref=packet.at[rows], dst_ref=arrived.at[rows], send_sem=z_sem.at[i], recv_sem=z_sem.at[2 + i],
+            device_id=opposite, device_id_type=MESH,
+        )
+
+    def arrivals(j, begin):
+        return [send[j, rank, begin : begin + 8]] + [recv[j, o, begin : begin + 8] for o in range(1, GROUP)]
+
+    def fact(o, i):
+        return traits[o, 0:1, i : i + 1]
+
+    def upper(j):
+        scores = [arrivals(j, 0), arrivals(j, 8)]
         peak = functools.reduce(jnp.maximum, scores[0] + scores[1])
         total = chirp_sum = delay_sum = jnp.zeros((8, 256), F32)
         for o in range(GROUP):
@@ -377,9 +368,12 @@
                 chirp_sum = chirp_sum + mass * fact(o, 1 + k)
                 delay_sum = delay_sum + mass * fact(o, 3 + k)
         inverse = 1.0 / total
-        upper = (peak + jnp.log(total), chirp_sum * inverse, delay_sum * inverse)
-
-        scores = arrivals(16)
+        return peak + jnp.log(total), chirp_sum * inverse, delay_sum * inverse
+
+    is_first = lax.broadcasted_iota(jnp.int32, (8, 256), 0) < 4
+
+    def lower(j):
+        scores = arrivals(j, 16)
         peak = functools.reduce(jnp.maximum, scores)
         peak = jnp.maximum(peak[:4], peak[4:])
         peak_twice = jnp.concatenate([peak, peak], axis=0)
@@ -391,28 +385,48 @@
             delay_sum = delay_sum + mass * jnp.where(is_first, fact(o, 3), fact(o, 4))
         total, chirp_sum, delay_sum = [v[:4] + v[4:] for v in (total, chirp_sum, delay_sum)]
         inverse = 1.0 / total
-        lower = (peak + jnp.log(total), chirp_sum * inverse, delay_sum * inverse)
-
-        for i, out in enumerate((mine_log, mine_chirp, mine_delay)):
-            for h in range(2):
-                lanes = slice(128 * h, 128 * h + 128)
-                if j == 0:
-                    packet[pl.ds(24 * i + h, 8, 2), :] = upper[i][:, lanes]
-                    packet[pl.ds(24 * i + 16 + h, 4, 2), :] = lower[i][:, lanes]
-                else:
-                    out[pl.ds(h, 8, 2), :] = upper[i][:, lanes]
-                    out[pl.ds(16 + h, 4, 2), :] = lower[i][:, lanes]
-        if j == 0:
-            z_copy.start()
+        return peak + jnp.log(total), chirp_sum * inverse, delay_sum * inverse
+
+    def landed(piece):
+        for o in range(1, GROUP):
+            score_copy(piece, o).wait_recv()
+
+    for copy in trait_copies:
+        copy.wait_recv()
+    traits[0] = trait[...]
+    landed(0)
+    for i, value in enumerate(upper(0)):
+        for h in range(2):
+            packet[pl.ds(16 * i + h, 8, 2), :] = value[:, 128 * h : 128 * h + 128]
+    z_copy(0).start()
+    weight_sum = fact(0, 0)
+    for o in range(1, GROUP):
+        weight_sum = weight_sum + fact(o, 0)
+    packet[72:80] = jnp.broadcast_to(weight_sum, (8, 128))
+    landed(1)
+    for o in (4, 5, 3, 2, 6, 7, 1):
+        score_copy(2, o).start()
+    for i, value in enumerate(lower(0)):
+        for h in range(2):
+            packet[pl.ds(48 + 8 * i + h, 4, 2), :] = value[:, 128 * h : 128 * h + 128]
+    z_copy(1).start()
+    landed(2)
+    for out, high, low in zip((mine_log, mine_chirp, mine_delay), upper(1), lower(1)):
+        for h in range(2):
+            lanes = slice(128 * h, 128 * h + 128)
+            out[pl.ds(h, 8, 2), :] = high[:, lanes]
+            out[pl.ds(16 + h, 4, 2), :] = low[:, lanes]
 
     for copy in trait_copies:
         copy.wait_send()
-    for j in range(HALVES):
+    for piece in range(3):
         for o in range(1, GROUP):
-            score_copy(j, o).wait_send()
-    z_copy.wait()
+            score_copy(piece, o).wait_send()
+    for i in range(2):
+        z_copy(i).wait()
     for i, out in enumerate((other_log, other_chirp, other_delay)):
-        out[...] = arrived[24 * i : 24 * i + 24]
+        out[0:16] = arrived[16 * i : 16 * i + 16]
+        out[16:24] = arrived[48 + 8 * i : 56 + 8 * i]
     level = jnp.log(packet[72:80] + arrived[72:80])
     for i in range(3):
         log_prior[8 * i : 8 * i + 8] = level
@@ -429,7 +443,7 @@
         out_shape=(
             pltpu.VMEM((512, 256), F32),
             pltpu.VMEM((2, 2, 128, 256), F32),
-            pltpu.VMEM((8, 128), F32),
+            pltpu.VMEM((1, 128), F32),
             pltpu.VMEM(base.shape, BF16),
             pltpu.VMEM(last.shape[1:], BF16),
             pltpu.VMEM(twist.shape, F32),
@@ -465,14 +479,14 @@
         scratch_shapes=[
             pltpu.VMEM((HALVES, GROUP, 24, 256), F32),
             pltpu.VMEM((HALVES, GROUP, 24, 256), F32),
-            pltpu.VMEM((GROUP, 8, 128), F32),
+            pltpu.VMEM((GROUP, 1, 128), F32),
             pltpu.VMEM((80, 128), F32),
             pltpu.VMEM((80, 128), F32),
-            dma((HALVES, GROUP)),
-            dma((HALVES, GROUP)),
+            dma((3, GROUP)),
+            dma((3, GROUP)),
             dma((GROUP,)),
             dma((GROUP,)),
-            dma((2,)),
+            dma((4,)),
         ],
         compiler_params=pltpu.CompilerParams(
             collective_id=1, has_side_effects=True, vmem_limit_bytes=56 * 1024 * 1024

time: 33.8 us -> 33.8 us (level)
  no operation moved by 1% of the time
where the time goes in v5:
time: 33.8 us; the launch traced here: 33.7 us
  Pallas kernels  32.4 us (96%)
  between operations  0.65 us (2%)
  other arithmetic  0.63 us (2%)
    pallas_call x1, Pallas kernels, local(): pl.pallas_call(match, out_shape=(pltpu.VMEM((24, 128), F32),) * 7, in_spe...  24.7 us
    pallas_call x1, Pallas kernels, local(): pl.pallas_call(prepare, out_shape=(pltpu.VMEM((512, 256), F32), pltpu.VME...  7.72 us

profile of v5, /device:TPU:32, one launch (start us, length us, event | category | flops | bytes accessed | tf_op | source)
XLA Modules:
  0.0 33.7 jit_solution(7512830946682071113)
XLA Ops:
  0.6 7.7 %shard_map.130 = (f32[512,256]{1,0:T(8,128)S(1)}, f32[2,2,128,256]{3,2,1,0:T(8,128)S(1)}, f32[1,128]{1,0:T(1,128)S(1)}, bf16[2,512,256]{2,1,0:T(8,128)(2,1)S(1)}...) custom-call(s32[2]{0:T(128)} %len_hbm.1, f32[2]{0:T(128)} %weight_hbm.1, f32[2]{0:T(128)} %mass_hbm.1, ...), custom_call_target="tpu_custom_call" | custom-call | tf_op jit(solution)/shard_map/pallas_call | solution.py:441
  8.4 24.7 %shard_map.131 = (f32[24,128]{1,0:T(8,128)S(1)}, f32[24,128]{1,0:T(8,128)S(1)}, f32[24,128]{1,0:T(8,128)S(1)}, f32[24,128]{1,0:T(8,128)S(1)}, f32[24,128]{1,0:T(...) custom-call(f32[512,256]{1,0:T(8,128)S(1)} %get-tuple-element.16.part, ...), custom_call_target="tpu_custom_call" | custom-call | tf_op jit(solution)/shard_map/pallas_call | solution.py:474
  33.0 0.6 %divide_bitcast_fusion = (f32[3072]{0:T(1024)}, f32[3072]{0:T(1024)}, f32[3072]{0:T(1024)}) fusion(f32[24,128]{1,0:T(8,128)S(1)} %get-tuple-element.28, f32[24,128]{1,0:T(8,128)S(1)} %get-tuple-element.27, f32[24,128]{1,0:T(8,128)S(1)} %get-tuple-element.22, f32[24,128]{1,0:T(8,128)S(1)} %get-tuple-element.23, f32[24,128]{1,0:T(8,128)S(1)} %get-tuple-element.24, ...), kind=kLoop, calls=%fused_computation | loop fusion | flops 43008 | bytes 122880 | tf_op jit(solution)/shard_map/reshape | solution.py:503

commit v6 on v4

--- a/solution.py
+++ b/solution.py
@@ -182,7 +182,7 @@
 
     for i in range(4, 7):
         loads[i].wait()
-    row = lax.broadcasted_iota(jnp.int32, (8, 128), 0)
+    lane = lax.broadcasted_iota(jnp.int32, (1, 128), 1)
     facts = (
         weight_ref[0] + weight_ref[1],
         mass_ref[0],
@@ -192,9 +192,9 @@
         weight_ref[0],
         weight_ref[1],
     )
-    tile = jnp.zeros((8, 128), F32)
+    tile = jnp.zeros((1, 128), F32)
     for i, fact in enumerate(facts):
-        tile = jnp.where(row == i, fact, tile)
+        tile = jnp.where(lane == i, fact, tile)
     trait[...] = tile
 
     loads[2].wait()
@@ -282,7 +282,6 @@
     spec = spec[:256] + spec[256:] + mul_t(second[0], low)
     spec_re, spec_im = spec[:128], spec[128:]
     third = thrice(*[turning(base[i, 0:256, 0:128], base[i, 256:512, 0:128]) for i in range(2)])
-    fourth = thrice(*[turning(last[i, 0:192], last[i, 192:384]) for i in range(2)])
     weights = []
     for k in range(2):
         filt_re, filt_im = filt[k, 0], filt[k, 1]
@@ -315,7 +314,7 @@
         )
         for o in range(1, GROUP)
     ]
-    log_weight = [jnp.log(jnp.broadcast_to(trait[5 + k : 6 + k, 0:1], (8, 256))) for k in range(2)]
+    log_weight = [jnp.log(jnp.broadcast_to(trait[0:1, 5 + k : 6 + k], (8, 256))) for k in range(2)]
     for j in range(HALVES):
         fourth = [turning(last[i, 96 * j : 96 * j + 96], last[i, 96 * j + 192 : 96 * j + 288]) for i in range(2)]
         stacked = jnp.concatenate(fourth, axis=0)
@@ -336,17 +335,17 @@
                 send[j, block + 1, 16 + 4 * k : 20 + 4 * k] = both[4:]
         if j == 0:
             pl.semaphore_wait(barrier, GROUP)
+            for o in (4, 5, 3, 2, 6, 7, 1):
+                score_copy(0, o).start()
             for copy in trait_copies:
                 copy.start()
-            for o in (4, 5, 3, 2, 6, 7, 1):
-                score_copy(0, o).start()
 
     for copy in trait_copies:
         copy.wait_recv()
     traits[0] = trait[...]
-    weight_sum = traits[0, 0:1, :]
+    weight_sum = traits[0, 0:1, 0:1]
     for o in range(1, GROUP):
-        weight_sum = weight_sum + traits[o, 0:1, :]
+        weight_sum = weight_sum + traits[o, 0:1, 0:1]
     packet[72:80] = jnp.broadcast_to(weight_sum, (8, 128))
 
     z_copy = pltpu.make_async_remote_copy(
@@ -365,7 +364,7 @@
             return [send[j, rank, begin : begin + 8]] + [recv[j, o, begin : begin + 8] for o in range(1, GROUP)]
 
         def fact(o, i):
-            return traits[o, i : i + 1, 0:1]
+            return traits[o, 0:1, i : i + 1]
 
         scores = [arrivals(0), arrivals(8)]
         peak = functools.reduce(jnp.maximum, scores[0] + scores[1])
@@ -429,7 +428,7 @@
         out_shape=(
             pltpu.VMEM((512, 256), F32),
             pltpu.VMEM((2, 2, 128, 256), F32),
-            pltpu.VMEM((8, 128), F32),
+            pltpu.VMEM((1, 128), F32),
             pltpu.VMEM(base.shape, BF16),
             pltpu.VMEM(last.shape[1:], BF16),
             pltpu.VMEM(twist.shape, F32),
@@ -465,7 +464,7 @@
         scratch_shapes=[
             pltpu.VMEM((HALVES, GROUP, 24, 256), F32),
             pltpu.VMEM((HALVES, GROUP, 24, 256), F32),
-            pltpu.VMEM((GROUP, 8, 128), F32),
+            pltpu.VMEM((GROUP, 1, 128), F32),
             pltpu.VMEM((80, 128), F32),
             pltpu.VMEM((80, 128), F32),
             dma((HALVES, GROUP)),

time: 33.8 us -> 34.1 us (level)
  Pallas kernels: 32.3 us -> 32.7 us
where the time goes in v6:
time: 34.1 us; the launch traced here: 34 us
  Pallas kernels  32.7 us (96%)
  between operations  0.65 us (2%)
  other arithmetic  0.63 us (2%)
    pallas_call x1, Pallas kernels, local(): pl.pallas_call(match, out_shape=(pltpu.VMEM((24, 128), F32),) * 7, in_spe...  25 us
    pallas_call x1, Pallas kernels, local(): pl.pallas_call(prepare, out_shape=(pltpu.VMEM((512, 256), F32), pltpu.VME...  7.72 us

profile of v6, /device:TPU:32, one launch (start us, length us, event | category | flops | bytes accessed | tf_op | source)
XLA Modules:
  0.0 34.0 jit_solution(1236674731591766191)
XLA Ops:
  0.6 7.7 %shard_map.130 = (f32[512,256]{1,0:T(8,128)S(1)}, f32[2,2,128,256]{3,2,1,0:T(8,128)S(1)}, f32[1,128]{1,0:T(1,128)S(1)}, bf16[2,512,256]{2,1,0:T(8,128)(2,1)S(1)}...) custom-call(s32[2]{0:T(128)} %len_hbm.1, f32[2]{0:T(128)} %weight_hbm.1, f32[2]{0:T(128)} %mass_hbm.1, ...), custom_call_target="tpu_custom_call" | custom-call | tf_op jit(solution)/shard_map/pallas_call | solution.py:426
  8.4 25.0 %shard_map.131 = (f32[24,128]{1,0:T(8,128)S(1)}, f32[24,128]{1,0:T(8,128)S(1)}, f32[24,128]{1,0:T(8,128)S(1)}, f32[24,128]{1,0:T(8,128)S(1)}, f32[24,128]{1,0:T(...) custom-call(f32[512,256]{1,0:T(8,128)S(1)} %get-tuple-element.16.part, ...), custom_call_target="tpu_custom_call" | custom-call | tf_op jit(solution)/shard_map/pallas_call | solution.py:459
  33.3 0.6 %divide_bitcast_fusion = (f32[3072]{0:T(1024)}, f32[3072]{0:T(1024)}, f32[3072]{0:T(1024)}) fusion(f32[24,128]{1,0:T(8,128)S(1)} %get-tuple-element.28, f32[24,128]{1,0:T(8,128)S(1)} %get-tuple-element.27, f32[24,128]{1,0:T(8,128)S(1)} %get-tuple-element.22, f32[24,128]{1,0:T(8,128)S(1)} %get-tuple-element.23, f32[24,128]{1,0:T(8,128)S(1)} %get-tuple-element.24, ...), kind=kLoop, calls=%fused_computation | loop fusion | flops 43008 | bytes 122880 | tf_op jit(solution)/shard_map/reshape | solution.py:488
